TPU v7x, 32 devices: a whole 2x2x4 slice. The times are simulated.
32 devices in a mesh: section: 2 (over core), ctx: 4 (over z), fsdp: 4 (over y, x).
Axes of the slice: x: 2, y: 2, z: 4, core: 2. Of those that a mesh axis runs over, the one named last changes fastest.
Arguments:
- inputs: bfloat16 [2, 4, 2048, 1024], P(None, 'fsdp', 'ctx'), may hold values from -6 to 6
- cotangent: bfloat16 [2, 4, 2048, 1024], P(None, 'fsdp', 'ctx'), may hold values from -6 to 6
- segments: int32 [2, 4, 2048], P(None, 'fsdp', 'ctx'), may hold values from 0 to 2047, as said below
- w_qkv: bfloat16 [2, 1024, 3072], P('section', 'fsdp'), may hold values from -0.1875 to 0.1875
- w_out: bfloat16 [2, 1024, 1024], P('section', 'fsdp'), may hold values from -0.5 to 0.5
- w_up: bfloat16 [2, 1024, 4096], P('section', 'fsdp'), may hold values from -0.1875 to 0.1875
- w_down: bfloat16 [2, 4096, 1024], P('section', 'fsdp'), may hold values from -0.09375 to 0.09375
- vectors: bfloat16 [2, 12288], P('section', 'fsdp'), may hold values from -0.8 to 1.25, as said below
Outputs:
- activations: bfloat16 [2, 2, 4, 2048, 1024], P('section', None, 'fsdp', 'ctx')
- input_grad: float32 [2, 2, 4, 2048, 1024], P('section', None, 'fsdp', 'ctx')
- grad_qkv: float32 [2, 1024, 3072], P('section', 'fsdp')
- grad_out: float32 [2, 1024, 1024], P('section', 'fsdp')
- grad_up: float32 [2, 1024, 4096], P('section', 'fsdp')
- grad_down: float32 [2, 4096, 1024], P('section', 'fsdp')
- grad_vectors: float32 [2, 12288], P('section', 'fsdp')
Inputs may be any that keep to these rules, and one draw needn't show every extreme that they name: `segments`: along a sequence the entries never fall and each is at most its own position; documents are contiguous. In every sequence slot of the micro-batches, one micro-batch drawn from the seed holds a single document over all 2048 positions. `vectors`: gains (entries 0 .. 1023 and 5120 .. 6143 of each section) lie in 0.75 to 1.25; the other entries are biases.
All inputs are finite; a program needn't handle non-finite values.
Results may differ from a plain program's by a relative error of at most 0.017.
Values may be sent and summed in bfloat16 or wider, within the bound.
No kernel may reach another device: no remote copies, remote signals or barrier semaphores. Data moves between devices by JAX's collectives and lax.ppermute only.
A program may use at most 640 MiB of HBM per device.

v0:
```python
import functools
import math

import jax
import jax.numpy as jnp
from jax import lax
from jax.experimental import pallas as pl
from jax.experimental.pallas import tpu as pltpu
from jax.sharding import PartitionSpec as P

D = 1024
HEADS = 16
FF = 4096
WIN = 1024

EPSILON = 1e-05
F32 = jnp.float32
BF16 = jnp.bfloat16
LANES = 128
MASKED = -1e30


LEAST = 256
ROLL = (3, 1, 2, 0)


def flip(block, axis, bit):
    count = lax.axis_size(axis)
    return lax.ppermute(block, axis, [(i, i ^ bit) for i in range(count)])


def step_along(block, axis, distance):
    devices = range(lax.axis_size(axis))
    route = [(i - distance, i) for i in devices if i - distance in devices]
    return lax.ppermute(block, axis, route)


def swap(block):
    return flip(block, "section", 1)


def tie(value, *after):
    return lax.optimization_barrier((value, after))[0]


class Gather:
    def __init__(self, shard, *after, then=()):
        shard = tie(shard, *after) if after else shard
        half = shard.shape[0] // 2
        self.near = flip(shard, "fsdp", 1), flip(shard, "fsdp", 2)
        from_x, from_y = tie(self.near, *then) if then else self.near
        self.far = flip(from_x[:half], "fsdp", 2), flip(from_y[half:], "fsdp", 1)
        self.pieces = (shard, *self.near, *self.far)


def add_bf16(*terms):
    return sum(term.astype(F32) for term in terms).astype(BF16)


class Scatter:
    def __init__(self, send_x, send_y, keep_x, keep_y):
        self.near = flip(send_x, "fsdp", 1), flip(send_y, "fsdp", 2)
        self.keep = keep_x, keep_y

    def second(self, *after):
        (got_x, got_y), (keep_x, keep_y) = tie(self.near, *after), self.keep
        self.half = add_bf16(keep_x[0], got_x[0]), add_bf16(keep_y[0], got_y[0])
        self.far = flip(self.half[0], "fsdp", 2), flip(self.half[1], "fsdp", 1)

    def third(self, *after):
        far_x, far_y = tie(self.far, *after)
        (got_x, got_y), (keep_x, keep_y) = self.near, self.keep
        self.piece = jnp.concatenate(
            [add_bf16(keep_x[1], got_x[1], far_x), add_bf16(keep_y[1], got_y[1], far_y)]
        )


class Column:
    def __init__(self):
        self.line = lax.axis_size("ctx") == 4
        me = lax.axis_index("ctx")
        self.inner = (me == 1) | (me == 2)
        self.block = self.half = self.total = self.outer_got = self.inner_got = None
        self.sums = []
        self.sent = ()

    def step(self, block, *after):
        if not self.line:
            if block is not None:
                self.sums.append(lax.psum(block, "ctx"))
            return
        outer_got, inner_got, block = tie((self.outer_got, self.inner_got, block), *after)
        half = total = None
        if self.block is not None:
            half = add_bf16(self.block, outer_got[: self.block.shape[0]])
        if self.half is not None:
            total = add_bf16(self.half, inner_got)
        if self.total is not None:
            outer_sum = outer_got[: self.total.shape[0]]
            self.sums.append(jnp.where(self.inner, self.total, outer_sum))
        self.block, self.half, self.total = block, half, total
        self.sent = ()
        if block is not None or total is not None:
            sent = total if block is None else block
            if block is not None and total is not None:
                rows = max(total.shape[0], block.shape[0])
                fill = lambda part: jnp.pad(part, ((0, rows - part.shape[0]), (0, 0)))
                sent = jnp.where(self.inner, fill(total), fill(block))
            self.outer_got = flip(sent, "ctx", 1)
            self.sent += (sent,)
        if half is not None:
            self.inner_got = lax.ppermute(half, "ctx", [(1, 2), (2, 1)])
            self.sent += (half,)


class Line:
    def __init__(self):
        self.token = ()
        self.also = ()

    def run(self, kernel, word, *args, after=()):
        word = tie(word, self.token, self.also, after)
        self.also = ()
        out = kernel(word, *args)
        self.token = out[0] if isinstance(out, (list, tuple)) else out
        return out


def sums_over_all(block):
    stages = [block]
    for axis in ("section", "fsdp", "ctx"):
        bit = 1
        while bit < lax.axis_size(axis):
            stages.append(stages[-1] + flip(stages[-1], axis, bit))
            bit *= 2
    return stages


def streamed(*arrays):
    return [pltpu.with_memory_space_constraint(array, pltpu.HBM) for array in arrays]


def call(kernel, out_shape, *operands, limit=28, flops=0, moved=0, exps=0, name=None, **rest):
    return pl.pallas_call(
        kernel,
        out_shape=out_shape,
        compiler_params=pltpu.CompilerParams(vmem_limit_bytes=limit * 1024 * 1024),
        cost_estimate=pl.CostEstimate(flops=flops, bytes_accessed=moved, transcendentals=exps),
        name=name,
        **rest,
    )(*operands)


def sds(*shape, dtype=BF16):
    return jax.ShapeDtypeStruct(shape, dtype)


def kept(*shape, dtype=BF16):
    return pltpu.HBM(shape, dtype)


ANYWHERE = pl.BlockSpec(memory_space=pltpu.HBM)
SCALARS = pl.BlockSpec(memory_space=pltpu.SMEM)
INSIDE = pl.BlockSpec(memory_space=pltpu.VMEM)


def fixed(*shape):
    return pl.BlockSpec(shape, lambda *_: (0,) * len(shape))


def fetches(me, pieces, wanted, sems):
    half = pieces[0].shape[0] // 2
    copies = []
    for number, (row, count, place) in enumerate(wanted):
        group = []
        for r in range(4):
            if r < 3:
                source = pieces[r].at[row : row + count]
            elif row < half:
                source = pieces[3].at[row : row + count]
            else:
                source = pieces[4].at[row - half : row - half + count]
            group.append(pltpu.make_async_copy(source, place(me ^ r), sems.at[number, r]))
        copies.append(group)
    return copies


def start_all(copies):
    for group in copies:
        for copy in group:
            copy.start()


def wait_group(group):
    for copy in group:
        copy.wait()


def part(a, size):
    return pl.ds(pl.multiple_of(a * size, size), size)


def wanted_qkv(w, which=(0, 1, 2)):
    return [
        (g * LEAST, LEAST, lambda a, i=i: w.at[i, part(a, LEAST)]) for i, g in enumerate(which)
    ]


def wanted_out(w):
    return [
        (3 * LEAST + j * 128, 128, lambda a, j=j: w.at[part(a, 128), j * 512 : (j + 1) * 512])
        for j in range(2)
    ]


def wanted_up(w):
    return [
        (j * LEAST, LEAST, lambda a, j=j: w.at[part(a, LEAST), j * 512 : (j + 1) * 512])
        for j in range(4)
    ]


def wanted_down(w):
    def place(a, rh, j):
        return w.at[pl.ds(pl.multiple_of(a * 512 + rh * 256, 256), 256), j * 512 : (j + 1) * 512]

    return [
        (
            (rh * 2 + j) * LEAST,
            LEAST,
            lambda a, rh=rh, j=j: place(a, rh, j),
        )
        for j in range(2)
        for rh in range(2)
    ]


def dot_nn(left, right):
    return lax.dot_general(left, right, (((1,), (0,)), ((), ())), preferred_element_type=F32)


def dot_nt(left, right):
    return lax.dot_general(left, right, (((1,), (1,)), ((), ())), preferred_element_type=F32)


def dot_tn(left, right):
    return lax.dot_general(left, right, (((0,), (0,)), ((), ())), preferred_element_type=F32)


def mean_last(values):
    return jnp.mean(values, axis=-1, keepdims=True)


def normalize(values):
    centred = values - mean_last(values)
    inverse = lax.rsqrt(mean_last(centred * centred) + EPSILON)
    return centred * inverse, inverse


def norm_back(grad_norm, normal, inverse):
    return inverse * (grad_norm - mean_last(grad_norm) - normal * mean_last(grad_norm * normal))


def column_sum(values):
    return jnp.sum(values.astype(F32), axis=0, keepdims=True)


def pack_kernel(
    core_ref, qkv, out, up, down, keep_a, send_a, keep_u, send_u, keep_d, send_d, sems
):
    core = core_ref[0]
    number = 0
    copies = []
    for target_a, target_u, target_d, half in (
        (send_a, send_u, send_d, 1 - core), (keep_a, keep_u, keep_d, core)
    ):
        for g in range(3):
            for f in range(4):
                columns = pl.ds(pl.multiple_of((g * 4 + f) * 256 + half * 128, 128), 128)
                copies.append(
                    (
                        qkv.at[0, :, columns],
                        target_a.at[g * LEAST : (g + 1) * LEAST, f * 128 : (f + 1) * 128],
                    )
                )
        for j in range(2):
            rows = pl.ds(pl.multiple_of(half * 128, 128), 128)
            copies.append(
                (
                    out.at[0, rows, j * 512 : (j + 1) * 512],
                    target_a.at[3 * LEAST + j * 128 : 3 * LEAST + (j + 1) * 128],
                )
            )
        for j in range(4):
            columns = pl.ds(pl.multiple_of(j * 1024 + half * 512, 512), 512)
            copies.append((up.at[0, :, columns], target_u.at[j * LEAST : (j + 1) * LEAST]))
        for rh in range(2):
            for j in range(2):
                rows = pl.ds(pl.multiple_of(half * 512 + rh * 256, 256), 256)
                at = (rh * 2 + j) * LEAST
                copies.append(
                    (down.at[0, rows, j * 512 : (j + 1) * 512], target_d.at[at : at + LEAST])
                )
    started = []
    for number, (source, target) in enumerate(copies):
        copy = pltpu.make_async_copy(source, target, sems.at[number])
        copy.start()
        started.append(copy)
    for copy in started:
        copy.wait()


def pack_weights(core, qkv, out, up, down):
    return call(
        pack_kernel,
        [kept(4 * LEAST, 512)] * 6,
        core, qkv, out, up, down,
        in_specs=[SCALARS] + [ANYWHERE] * 4,
        out_specs=[ANYWHERE] * 6,
        scratch_shapes=[pltpu.SemaphoreType.DMA((44,))],
        moved=12 << 20,
        limit=16,
        name="pack_weights",
    )


def qkv_kernel(
    me_ref, own_ref, other_ref, gain, bias, bq, bv, w0, w1, w2, w3, w4,
    a_ref, q_ref, k_ref, v_ref, w, sems,
):
    copies = fetches(me_ref[0], (w0, w1, w2, w3, w4), wanted_qkv(w), sems)
    start_all(copies)
    scale = BF16(1.0 / math.sqrt(D // HEADS))
    for m, x_ref in enumerate((own_ref, other_ref)):
        normed = (normalize(x_ref[...].astype(F32))[0] * gain[...] + bias[...]).astype(BF16)
        a_ref[m] = normed
        if m == 0:
            for group in copies:
                wait_group(group)
        q_ref[m] = (dot_nn(normed, w[0]) + bq[...]).astype(BF16) * scale
        k_ref[m] = dot_nn(normed, w[1]).astype(BF16)
        v_ref[m] = (dot_nn(normed, w[2]) + bv[...]).astype(BF16)


def make_qkv(me, own, other, gain, bias, bq, bv, pieces):
    rows = own.shape[0]
    half = D // 2
    return call(
        qkv_kernel,
        [kept(2, rows, D)] + [kept(2, rows, half)] * 3,
        me, own, other, gain, bias, bq, bv, *pieces,
        grid=(1,),
        in_specs=[SCALARS, fixed(rows, D), fixed(rows, D)]
        + [fixed(1, D), fixed(1, D), fixed(1, half), fixed(1, half)]
        + [ANYWHERE] * 5,
        out_specs=[fixed(2, rows, D)] + [fixed(2, rows, half)] * 3,
        scratch_shapes=[pltpu.VMEM((3, D, half), BF16), pltpu.SemaphoreType.DMA((3, 4))],
        flops=4 * rows * D * 3 * half,
        moved=14 << 20,
        name="project_qkv",
    )


def kv_kernel(me_ref, own_ref, other_ref, gain, bias, bv, w0, w1, w2, w3, w4, *rest):
    a_ref, k_ref, v_ref, w, sems = rest[-5:]
    copies = fetches(me_ref[0], (w0, w1, w2, w3, w4), wanted_qkv(w, (1, 2)), sems)
    start_all(copies)
    for m, x_ref in enumerate((own_ref, other_ref)):
        normed = (normalize(x_ref[...].astype(F32))[0] * gain[...] + bias[...]).astype(BF16)
        a_ref[m] = normed
        if m == 0:
            for group in copies:
                wait_group(group)
        k_ref[m] = dot_nn(normed, w[0]).astype(BF16)
        v_ref[m] = (dot_nn(normed, w[1]) + bv[...]).astype(BF16)


def make_kv(me, own, other, hops, at, earlier, gain, bias, bv, pieces):
    rows = own.shape[0]
    halo = hops * rows
    half = D // 2
    row = lambda width: pl.BlockSpec((2, rows, width), lambda i: (0, at, 0))
    first = 11
    return call(
        kv_kernel,
        [kept(2, halo, D), kept(2, halo, half), kept(2, halo, half)],
        me, own, other, gain, bias, bv, *pieces, *earlier,
        grid=(1,),
        in_specs=[SCALARS, fixed(rows, D), fixed(rows, D), fixed(1, D), fixed(1, D), fixed(1, half)]
        + [ANYWHERE] * 5
        + [ANYWHERE] * len(earlier),
        out_specs=[row(D), row(half), row(half)],
        input_output_aliases={first + i: i for i in range(len(earlier))},
        scratch_shapes=[pltpu.VMEM((2, D, half), BF16), pltpu.SemaphoreType.DMA((2, 4))],
        flops=2 * 2 * rows * D * 2 * half,
        moved=8 << 20,
        name="project_earlier",
    )


def out_kernel(me_ref, o_ref, w0, w1, w2, w3, w4, p_ref, w, sems):
    copies = fetches(me_ref[0], (w0, w1, w2, w3, w4), wanted_out(w), sems)
    start_all(copies)
    for group in copies:
        wait_group(group)
    p_ref[...] = dot_nn(o_ref[0], w[...]).astype(BF16)


def out_other(me, o, pieces):
    _, rows, half = o.shape
    return call(
        out_kernel,
        sds(rows, D),
        me, o, *pieces,
        grid=(1,),
        in_specs=[SCALARS, fixed(1, rows, half)] + [ANYWHERE] * 5,
        out_specs=fixed(rows, D),
        scratch_shapes=[pltpu.VMEM((half, D), BF16), pltpu.SemaphoreType.DMA((2, 4))],
        flops=2 * rows * half * D,
        moved=3 << 20,
        name="out_other",
    )


def middle_kernel(
    me_ref, o_ref, got, x_ref, bo, gain, bias, w0, w1, w2, w3, w4, x1_ref, h_ref, w, sems
):
    copies = fetches(me_ref[0], (w0, w1, w2, w3, w4), wanted_out(w), sems)
    start_all(copies)
    base = x_ref[...].astype(F32) + got[...].astype(F32) + bo[...]
    for group in copies:
        wait_group(group)
    x1 = base + dot_nn(o_ref[0], w[...])
    x1_ref[...] = x1
    h_ref[...] = (normalize(x1)[0] * gain[...] + bias[...]).astype(BF16)


def middle(me, o, got, x, bo, gain, bias, pieces):
    _, rows, half = o.shape
    return call(
        middle_kernel,
        [sds(rows, D, dtype=F32), sds(rows, D)],
        me, o, got, x, bo, gain, bias, *pieces,
        grid=(1,),
        in_specs=[SCALARS, fixed(1, rows, half)]
        + [fixed(rows, D)] * 2
        + [fixed(1, D)] * 3
        + [ANYWHERE] * 5,
        out_specs=[fixed(rows, D)] * 2,
        scratch_shapes=[pltpu.VMEM((half, D), BF16), pltpu.SemaphoreType.DMA((2, 4))],
        flops=2 * rows * half * D,
        moved=8 << 20,
        name="middle",
    )


def gelu_and_slope(u):
    c = math.sqrt(2.0 / math.pi)
    square = u * u
    half = 0.5 + 0.5 * jnp.tanh(u * (c + (c * 0.044715) * square))
    value = u * half
    slope = half + value * (1.0 - half) * (2.0 * c + (6.0 * c * 0.044715) * square)
    return value, slope


def up_kernel(me_ref, h_ref, bu, w0, w1, w2, w3, w4, act_ref, slope_ref, w, sems):
    copies = fetches(me_ref[0], (w0, w1, w2, w3, w4), wanted_up(w), sems)
    step = pl.program_id(0)

    @pl.when(step == 0)
    def _():
        start_all(copies)

    for j in range(4):

        @pl.when(step == j)
        def _(j=j):
            wait_group(copies[j])
            columns = slice(j * 512, (j + 1) * 512)
            rows = h_ref.shape[0]
            piece = min(256, rows)
            for r in range(0, rows, piece):
                u = dot_nn(h_ref[r : r + piece], w[:, columns]) + bu[:, columns]
                value, slope = gelu_and_slope(u)
                act_ref[r : r + piece] = value.astype(BF16)
                slope_ref[r : r + piece] = slope.astype(BF16)


def up(me, h, bu, pieces):
    rows = h.shape[0]
    half = FF // 2
    out = pl.BlockSpec((rows, 512), lambda j: (0, j))
    return call(
        up_kernel,
        [sds(rows, half), kept(rows, half)],
        me, h, bu, *pieces,
        grid=(4,),
        in_specs=[SCALARS, fixed(rows, D), fixed(1, half)] + [ANYWHERE] * 5,
        out_specs=[out, out],
        scratch_shapes=[pltpu.VMEM((D, half), BF16), pltpu.SemaphoreType.DMA((4, 4))],
        flops=2 * rows * half * D,
        moved=9 << 20,
        exps=rows * half,
        name="up",
    )


def down_kernel(me_ref, act, w0, w1, w2, w3, w4, p_ref, w, sems):
    copies = fetches(me_ref[0], (w0, w1, w2, w3, w4), wanted_down(w), sems)
    start_all(copies)
    for j in range(2):
        wait_group(copies[2 * j])
        wait_group(copies[2 * j + 1])
        columns = slice(j * 512, (j + 1) * 512)
        p_ref[:, columns] = dot_nn(act[...], w[:, columns]).astype(BF16)


def down_other(me, act, pieces):
    rows, half = act.shape
    return call(
        down_kernel,
        sds(rows, D),
        me, act, *pieces,
        grid=(1,),
        in_specs=[SCALARS, fixed(rows, half)] + [ANYWHERE] * 5,
        out_specs=fixed(rows, D),
        scratch_shapes=[pltpu.VMEM((half, D), BF16), pltpu.SemaphoreType.DMA((4, 4))],
        flops=2 * rows * half * D,
        moved=7 << 20,
        name="down_other",
    )


def last_kernel(me_ref, act, got, x1, bd, w0, w1, w2, w3, w4, y_ref, w, sems):
    copies = fetches(me_ref[0], (w0, w1, w2, w3, w4), wanted_down(w), sems)
    start_all(copies)
    for j in range(2):
        wait_group(copies[2 * j])
        wait_group(copies[2 * j + 1])
        columns = slice(j * 512, (j + 1) * 512)
        base = x1[:, columns] + got[:, columns].astype(F32) + bd[:, columns]
        y_ref[:, columns] = (base + dot_nn(act[...], w[:, columns])).astype(BF16)


def last(me, act, got, x1, bd, pieces):
    rows, half = act.shape
    return call(
        last_kernel,
        sds(rows, D),
        me, act, got, x1, bd, *pieces,
        grid=(1,),
        in_specs=[SCALARS, fixed(rows, half), fixed(rows, D), fixed(rows, D), fixed(1, D)]
        + [ANYWHERE] * 5,
        out_specs=fixed(rows, D),
        scratch_shapes=[pltpu.VMEM((half, D), BF16), pltpu.SemaphoreType.DMA((4, 4))],
        flops=2 * rows * half * D,
        moved=10 << 20,
        name="down_own",
    )


def lanes_of(rows, low):
    lane = lax.broadcasted_iota(jnp.int32, (rows, LANES), 1)
    return lane < LANES // 2 if low else lane >= LANES // 2


def split3(values):
    first = values.astype(BF16)
    rest = values - first.astype(F32)
    second = rest.astype(BF16)
    third = (rest - second.astype(F32)).astype(BF16)
    return first, second, third


def forward_kernel(
    rows, halo, block,
    word, q_ref, kh_ref, ko_ref, vh_ref, vo_ref, lo_ref, ek_ref, eq_ref, o_ref, e_ref,
):
    lane = lax.broadcasted_iota(jnp.int32, (block, LANES), 1)
    for q0 in range(0, rows, block):
        k0 = max(0, halo + q0 - WIN) // block * block
        k1 = halo + q0 + block
        q = q_ref[0, q0 : q0 + block, :]
        lo = lo_ref[0, q0 : q0 + block, :]
        outs = []
        for t in range(2):
            keep = lanes_of(block, t == 0)
            eq = jnp.broadcast_to(eq_ref[0, t : t + 1, :], (block, LANES))
            qcat = jnp.concatenate([q, eq.astype(BF16)], axis=1)
            tiles = []
            for kb in range(k0, k1, block):
                k = kh_ref[0, kb : kb + block, :] if kb < halo else ko_ref[0, kb - halo : kb - halo + block, :]
                kcat = jnp.concatenate(
                    [jnp.where(keep, k, jnp.zeros_like(k)), ek_ref[kb : kb + block, :]], axis=1
                )
                s = dot_nt(qcat, kcat)
                kidx = lax.broadcasted_iota(jnp.int32, (block, block), 1) + kb
                allowed = kidx >= lo
                if kb + block == k1:
                    qidx = lax.broadcasted_iota(jnp.int32, (block, block), 0) + (halo + q0)
                    allowed = allowed & (kidx <= qidx)
                tiles.append(jnp.where(allowed, s, MASKED))
            top = functools.reduce(jnp.maximum, tiles)
            m = jnp.max(top, axis=1, keepdims=True)
            product = None
            for kb, s in zip(range(k0, k1, block), tiles):
                if kb < halo:
                    v = vh_ref[0, kb : kb + block, :]
                else:
                    v = vo_ref[0, kb - halo : kb - halo + block, :]
                part = dot_nn(
                    jnp.exp(s - m).astype(BF16), jnp.concatenate([v, jnp.ones_like(v)], axis=1)
                )
                product = part if product is None else product + part
            total = product[:, LANES : LANES + 1]
            outs.append(product[:, :LANES] / total)
            first, second, third = split3(-(m + jnp.log(total)))
            e = jnp.where(lane == 6, first.astype(F32), eq)
            e = jnp.where(lane == 7, second.astype(F32), e)
            e = jnp.where(lane == 8, third.astype(F32), e)
            e_ref[0, t, q0 : q0 + block, :] = e.astype(BF16)
        o_ref[0, q0 : q0 + block, :] = jnp.where(lanes_of(block, True), outs[0], outs[1]).astype(
            BF16
        )


def attend(word, which, q, kh, ko, vh, vo, lo, ek, eq):
    _, rows, width = q.shape
    halo = kh.shape[1]
    pairs = width // LANES
    block = min(256, rows)
    spec = lambda n: pl.BlockSpec((1, n, LANES), lambda p: (which, 0, p))
    count = pairs * 2 * rows * (WIN + block)
    return call(
        functools.partial(forward_kernel, rows, halo, block),
        [sds(1, rows, width), kept(1, 2 * pairs, rows, LANES)],
        word, *streamed(q, kh, ko, vh, vo), lo, ek, eq,
        grid=(pairs,),
        in_specs=[
            SCALARS,
            spec(rows), spec(halo), spec(rows), spec(halo), spec(rows),
            pl.BlockSpec((1, rows, 1), lambda p: (which, 0, 0)),
            fixed(halo + rows, LANES),
            pl.BlockSpec((1, 2, LANES), lambda p: (p, 0, 0)),
        ],
        out_specs=[
            pl.BlockSpec((1, rows, LANES), lambda p: (0, 0, p)),
            pl.BlockSpec((1, 2, rows, LANES), lambda p: (0, p, 0, 0)),
        ],
        flops=count * 1024,
        moved=6 << 20,
        exps=count,
        name="attention_forward",
    )


def backward_kernel(
    rows, halo, block, begin, end, final,
    word, q_ref, kh_ref, ko_ref, vh_ref, vo_ref, o_ref, do_ref, e_ref, lo_ref, ek_ref, *refs,
):
    acc_ref = refs[-1]
    refs = list(refs[:-1])
    start_ref = refs.pop(0) if begin > 0 else None
    dq_ref = refs.pop(0)
    dkh_ref, dvh_ref = (refs.pop(0), refs.pop(0)) if begin == 0 else (None, None)
    dko_ref, dvo_ref = (refs.pop(0), refs.pop(0)) if final else (None, None)
    q = q_ref[0]
    do = do_ref[0]
    lo = lo_ref[0]
    lane = lax.broadcasted_iota(jnp.int32, (rows, LANES), 1)
    ones = jnp.where(lax.broadcasted_iota(jnp.int32, (block, LANES), 1) < 3, 1.0, 0.0).astype(BF16)
    product = do.astype(F32) * o_ref[0].astype(F32)
    qcats, docats, qts, dots = [], [], [], []
    for t in range(2):
        keep = lanes_of(rows, t == 0)
        delta = jnp.sum(jnp.where(keep, product, 0.0), axis=1, keepdims=True)
        first, second, third = split3(-delta)
        ed = jnp.where(lane == 0, first.astype(F32), 0.0)
        ed = jnp.where(lane == 1, second.astype(F32), ed)
        ed = jnp.where(lane == 2, third.astype(F32), ed)
        qcats.append(jnp.concatenate([q, e_ref[0, t]], axis=1))
        docats.append(jnp.concatenate([do, ed.astype(BF16)], axis=1))
        qts.append(jnp.where(keep, q, jnp.zeros_like(q)))
        dots.append(jnp.where(keep, do, jnp.zeros_like(do)))
    acc_ref[...] = jnp.zeros_like(acc_ref) if start_ref is None else start_ref[0]
    for kb in range(begin, end, block):
        if kb < halo:
            k_in, v_in, dk_out, dv_out, at = kh_ref, vh_ref, dkh_ref, dvh_ref, kb
        else:
            k_in, v_in, dk_out, dv_out, at = ko_ref, vo_ref, dko_ref, dvo_ref, kb - halo
        qlo = max(0, kb - halo)
        qhi = min(rows, -(-(kb + block - 1 + WIN - halo) // block) * block)
        if qhi <= qlo:
            dk_out[0, at : at + block, :] = jnp.zeros((block, LANES), BF16)
            dv_out[0, at : at + block, :] = jnp.zeros((block, LANES), BF16)
            continue
        k = k_in[0, at : at + block, :]
        v = v_in[0, at : at + block, :]
        ek = ek_ref[kb : kb + block, :]
        kidx = lax.broadcasted_iota(jnp.int32, (block, qhi - qlo), 0) + kb
        allowed = kidx >= lo[:, qlo:qhi]
        if kb + block > halo + qlo:
            qidx = lax.broadcasted_iota(jnp.int32, (block, qhi - qlo), 1) + (halo + qlo)
            allowed = allowed & (kidx <= qidx)
        pts, dss, kts = [], [], []
        for t in range(2):
            keep = lanes_of(block, t == 0)
            kt = jnp.where(keep, k, jnp.zeros_like(k))
            vt = jnp.where(keep, v, jnp.zeros_like(v))
            st = dot_nt(jnp.concatenate([kt, ek], axis=1), qcats[t][qlo:qhi])
            pt = jnp.exp(jnp.where(allowed, st, MASKED))
            dpt = dot_nt(jnp.concatenate([vt, ones], axis=1), docats[t][qlo:qhi])
            pts.append(pt.astype(BF16))
            dss.append((pt * dpt).astype(BF16))
            kts.append(kt)
        dv = dot_nn(jnp.concatenate(pts, axis=1), jnp.concatenate([d[qlo:qhi] for d in dots], axis=0))
        dk = dot_nn(jnp.concatenate(dss, axis=1), jnp.concatenate([d[qlo:qhi] for d in qts], axis=0))
        dv_out[0, at : at + block, :] = dv.astype(BF16)
        dk_out[0, at : at + block, :] = dk.astype(BF16)
        acc_ref[:, qlo:qhi] += dot_tn(jnp.concatenate(kts, axis=0), jnp.concatenate(dss, axis=0))
    if final:
        scale = 1.0 / math.sqrt(LANES // 2)
        dq_ref[0] = (acc_ref[...].T * scale).astype(BF16)
    else:
        dq_ref[0] = acc_ref[...]


def attend_back(word, which, q, kh, ko, vh, vo, o, do, e, lo, ek, start=None):
    _, rows, width = q.shape
    halo = kh.shape[1]
    pairs = width // LANES
    block = min(256, rows)
    begin, end, final = (0, halo, False) if start is None else (halo, halo + rows, True)
    spec = lambda n: pl.BlockSpec((1, n, LANES), lambda p: (which, 0, p))
    only = lambda n: pl.BlockSpec((1, n, LANES), lambda p: (0, 0, p))
    sums = pl.BlockSpec((1, LANES, rows), lambda p: (0, p, 0))
    count = pairs * 2 * rows * (WIN + block) * (end - begin) // (halo + rows)
    if final:
        shapes, specs = [sds(1, rows, width)] * 3, [only(rows)] * 3
    else:
        shapes = [sds(1, width, rows, dtype=F32)] + [sds(1, halo, width)] * 2
        specs = [sums, only(halo), only(halo)]
    return call(
        functools.partial(backward_kernel, rows, halo, block, begin, end, final),
        shapes,
        word, *streamed(q, kh, ko, vh, vo), o, do, *streamed(e), lo, ek,
        *([] if start is None else [start]),
        grid=(pairs,),
        in_specs=[
            SCALARS,
            spec(rows), spec(halo), spec(rows), spec(halo), spec(rows), only(rows), spec(rows),
            pl.BlockSpec((1, 2, rows, LANES), lambda p: (0, p, 0, 0)),
            pl.BlockSpec((1, 1, rows), lambda p: (which, 0, 0)),
            fixed(halo + rows, LANES),
        ]
        + ([] if start is None else [sums]),
        out_specs=specs,
        scratch_shapes=[pltpu.VMEM((LANES, rows), F32)],
        flops=count * 2304,
        moved=8 << 20,
        exps=count,
        name="attention_backward",
    )


def act_back_kernel(
    me_ref, own, other, slope_own, slope_other, w0, w1, w2, w3, w4,
    du_own, du_other, sums, w, sems,
):
    copies = fetches(me_ref[0], (w0, w1, w2, w3, w4), wanted_down(w), sems)
    step = pl.program_id(0)

    @pl.when(step == 0)
    def _():
        start_all(copies)
        for group in copies:
            wait_group(group)

    rows = own.shape[0]
    piece = min(256, rows)
    w_part = w[pl.ds(pl.multiple_of(step * 512, 512), 512), :]
    total = jnp.zeros((1, 512), F32)
    for dy, slope, du in ((other, slope_other, du_other), (own, slope_own, du_own)):
        for r in range(0, rows, piece):
            grad = dot_nt(dy[r : r + piece], w_part) * slope[r : r + piece].astype(F32)
            rounded = grad.astype(BF16)
            du[r : r + piece] = rounded
            total += column_sum(rounded)
    sums[...] = jnp.broadcast_to(total, (8, 512))


def act_back(me, own, other, slope_own, slope_other, pieces):
    rows = own.shape[0]
    half = FF // 2
    columns = pl.BlockSpec((rows, 512), lambda j: (0, j))
    return call(
        act_back_kernel,
        [sds(rows, half), sds(rows, half), sds(8, half, dtype=F32)],
        me, own, other, *streamed(slope_own, slope_other), *pieces,
        grid=(4,),
        in_specs=[SCALARS, fixed(rows, D), fixed(rows, D), columns, columns] + [ANYWHERE] * 5,
        out_specs=[columns, columns, pl.BlockSpec((8, 512), lambda j: (0, j))],
        scratch_shapes=[pltpu.VMEM((half, D), BF16), pltpu.SemaphoreType.DMA((4, 4))],
        flops=4 * rows * half * D,
        moved=16 << 20,
        name="act_back",
    )


def up_back_kernel(me_ref, du, w0, w1, w2, w3, w4, p_ref, w, sems):
    copies = fetches(me_ref[0], (w0, w1, w2, w3, w4), wanted_up(w), sems)
    start_all(copies)
    for group in copies:
        wait_group(group)
    p_ref[...] = dot_nt(du[...], w[...]).astype(BF16)


def up_back_other(me, du, pieces):
    rows, half = du.shape
    return call(
        up_back_kernel,
        sds(rows, D),
        me, du, *pieces,
        grid=(1,),
        in_specs=[SCALARS, fixed(rows, half)] + [ANYWHERE] * 5,
        out_specs=fixed(rows, D),
        scratch_shapes=[pltpu.VMEM((D, half), BF16), pltpu.SemaphoreType.DMA((4, 4))],
        flops=2 * rows * half * D,
        moved=7 << 20,
        name="up_back_other",
    )


def middle_back_kernel(
    me_ref, du, got, x1, dy, gain, w0, w1, w2, w3, w4, dx1_ref, db_ref, sums, w, sems
):
    copies = fetches(me_ref[0], (w0, w1, w2, w3, w4), wanted_up(w), sems)
    start_all(copies)
    normal, inverse = normalize(x1[...])
    for group in copies:
        wait_group(group)
    dh = dot_nt(du[...], w[...]) + got[...].astype(F32)
    top = dy[...].astype(F32)
    dx1 = top + norm_back(dh * gain[...], normal, inverse)
    dx1_ref[...] = dx1
    db = dx1.astype(BF16)
    db_ref[...] = db
    sums[0:1] = column_sum(dh * normal)
    sums[1:2] = column_sum(dh)
    sums[2:3] = column_sum(db)
    sums[3:4] = column_sum(top)
    sums[4:8] = jnp.zeros((4, D), F32)


def middle_back(me, du, got, x1, dy, gain, pieces):
    rows, half = du.shape
    return call(
        middle_back_kernel,
        [sds(rows, D, dtype=F32), sds(rows, D), sds(8, D, dtype=F32)],
        me, du, got, x1, dy, gain, *pieces,
        grid=(1,),
        in_specs=[SCALARS, fixed(rows, half)]
        + [fixed(rows, D)] * 3
        + [fixed(1, D)]
        + [ANYWHERE] * 5,
        out_specs=[fixed(rows, D), fixed(rows, D), fixed(8, D)],
        scratch_shapes=[pltpu.VMEM((D, half), BF16), pltpu.SemaphoreType.DMA((4, 4))],
        flops=2 * rows * half * D,
        moved=14 << 20,
        name="middle_back",
    )


def out_back_kernel(me_ref, own, other, w0, w1, w2, w3, w4, do_ref, w, sems):
    copies = fetches(me_ref[0], (w0, w1, w2, w3, w4), wanted_out(w), sems)
    start_all(copies)
    for group in copies:
        wait_group(group)
    do_ref[0] = dot_nt(own[...], w[...]).astype(BF16)
    do_ref[1] = dot_nt(other[...], w[...]).astype(BF16)


def out_back(me, own, other, pieces):
    rows = own.shape[0]
    half = D // 2
    return call(
        out_back_kernel,
        sds(2, rows, half),
        me, own, other, *pieces,
        grid=(1,),
        in_specs=[SCALARS, fixed(rows, D), fixed(rows, D)] + [ANYWHERE] * 5,
        out_specs=fixed(2, rows, half),
        scratch_shapes=[pltpu.VMEM((half, D), BF16), pltpu.SemaphoreType.DMA((2, 4))],
        flops=4 * rows * half * D,
        moved=4 << 20,
        name="out_back",
    )


def store_parts(step, parts_x, parts_y, send_x, send_y, keep_x, keep_y):
    def put(ref, pieces):
        row = 0
        for piece in pieces:
            ref[0, row : row + piece.shape[0]] = piece
            row += piece.shape[0]

    @pl.when(step < 2)
    def _():
        put(send_x, parts_x)

    @pl.when(step >= 2)
    def _():
        put(keep_x, parts_x)

    @pl.when(step % 2 == 0)
    def _():
        put(send_y, parts_y)

    @pl.when(step % 2 == 1)
    def _():
        put(keep_y, parts_y)


def part_outputs(rows):
    shapes = [kept(2, rows, 512)] * 4
    specs = [
        pl.BlockSpec((1, rows, 512), lambda i, order: (jnp.minimum(i, 1), 0, 0)),
        pl.BlockSpec((1, rows, 512), lambda i, order: (i // 2, 0, 0)),
        pl.BlockSpec((1, rows, 512), lambda i, order: (i // 3, 0, 0)),
        pl.BlockSpec((1, rows, 512), lambda i, order: (i // 3, 0, 0)),
    ]
    return shapes, specs


def down_grad_kernel(order, act_own, act_other, own, other, *outs):
    grad = (dot_tn(act_own[...], own[...]) + dot_tn(act_other[...], other[...])).astype(BF16)
    store_parts(
        pl.program_id(0),
        [grad[:256, :512], grad[:256, 512:]],
        [grad[256:, :512], grad[256:, 512:]],
        *outs,
    )


def down_grad(order, act_own, act_other, own, other):
    rows = own.shape[0]
    shapes, specs = part_outputs(512)
    columns = pl.BlockSpec((rows, 512), lambda i, order: (0, order[i]))
    full = pl.BlockSpec((rows, D), lambda i, order: (0, 0))
    return call(
        down_grad_kernel,
        shapes,
        order, *streamed(act_own, act_other), own, other,
        grid_spec=pltpu.PrefetchScalarGridSpec(
            num_scalar_prefetch=1,
            grid=(4,),
            in_specs=[columns, columns, full, full],
            out_specs=specs,
        ),
        flops=4 * rows * (FF // 2) * D,
        moved=10 << 20,
        name="down_grad",
    )


def up_grad_kernel(
    order, h_own, h_other, du_own, du_other, o_own, o_other, db_own, db_other, *outs
):
    grad = (dot_tn(h_own[...], du_own[...]) + dot_tn(h_other[...], du_other[...])).astype(BF16)
    out_part = (dot_tn(o_own[0], db_own[...]) + dot_tn(o_other[0], db_other[...])).astype(BF16)
    store_parts(
        pl.program_id(0),
        [grad[:, :512], grad[:, 512:1024], out_part[:, :512]],
        [grad[:, 1024:1536], grad[:, 1536:], out_part[:, 512:]],
        *outs,
    )


def up_grad(order, h_own, h_other, du_own, du_other, o_own, o_other, db_own, db_other):
    rows = h_own.shape[0]
    half = FF // 2
    shapes, specs = part_outputs(640)
    columns = pl.BlockSpec((rows, 256), lambda i, order: (0, order[i]))
    full = lambda width: pl.BlockSpec((rows, width), lambda i, order: (0, 0))
    heads = pl.BlockSpec((1, rows, 128), lambda i, order: (0, 0, order[i]))
    return call(
        up_grad_kernel,
        shapes,
        order, h_own, h_other, du_own, du_other, o_own, o_other, db_own, db_other,
        grid_spec=pltpu.PrefetchScalarGridSpec(
            num_scalar_prefetch=1,
            grid=(4,),
            in_specs=[columns, columns, full(half), full(half), heads, heads, full(D), full(D)],
            out_specs=specs,
        ),
        flops=4 * rows * half * D + 2 * rows * D * D,
        moved=14 << 20,
        name="up_grad",
    )


def qkv_grad_kernel(order, a_own, a_halo, *refs):
    dq, dko, dvo, dkh, dvh = (refs[2 * i : 2 * i + 2] for i in range(5))
    *parts, sums = refs[10:]

    def total(pairs):
        return sum(dot_tn(left[m], right[m][0]) for left, right in pairs for m in range(2)).astype(BF16)

    k_part = total([(a_own, dko), (a_halo, dkh)])
    first = [total([(a_own, dq)]), k_part[:128]]
    second = [k_part[128:], total([(a_own, dvo), (a_halo, dvh)])]
    store_parts(pl.program_id(0), first, second, *parts)

    @pl.when(pl.program_id(0) == 0)
    def _():
        sums[0:1] = column_sum(dq[0][0]) + column_sum(dq[1][0])
        sums[1:2] = sum(column_sum(ref[0]) for ref in (*dvo, *dvh))
        sums[2:8] = jnp.zeros((6, sums.shape[1]), F32)


def qkv_grad(order, a_own, a_halo, *grads):
    rows, halo = a_own.shape[1], a_halo.shape[1]
    half = D // 2
    shapes, specs = part_outputs(384)
    full = lambda n: pl.BlockSpec((1, n, half), lambda i, order: (0, 0, 0))
    columns = lambda n: pl.BlockSpec((2, n, 256), lambda i, order: (0, 0, order[i]))
    return call(
        qkv_grad_kernel,
        shapes + [sds(8, half, dtype=F32)],
        order, a_own, a_halo, *[ref for pair in grads for ref in pair],
        grid_spec=pltpu.PrefetchScalarGridSpec(
            num_scalar_prefetch=1,
            grid=(4,),
            in_specs=[columns(rows), columns(halo)]
            + [full(rows)] * 6
            + [full(halo)] * 4,
            out_specs=specs + [pl.BlockSpec((8, half), lambda i, order: (0, 0))],
        ),
        flops=4 * D * half * (3 * rows + 2 * halo),
        moved=16 << 20,
        name="qkv_grad",
    )


def normed_back_kernel(hops, me_ref, *refs):
    wanted = (1, 2) if hops else (0, 1, 2)
    count = len(wanted)
    grads, a_ref, refs = refs[:count], refs[count], refs[count + 1 :]
    *outs, sums, w, sems = refs[5:]
    got = outs.pop(0) if len(outs) > max(hops, 1) else None
    copies = fetches(me_ref[0], refs[:5], wanted_qkv(w, wanted), sems)
    start_all(copies)
    for group in copies:
        wait_group(group)
    weighted = jnp.zeros((1, D), F32)
    plain = jnp.zeros((1, D), F32)
    rows = outs[0].shape[0] if got is not None else a_ref.shape[1] // max(hops, 1)
    for number in range(max(hops, 1)):
        r = slice(number * rows, (number + 1) * rows)
        da = sum(dot_nt(grad[0, r], w[i]) for i, grad in enumerate(grads))
        weighted += column_sum(da * a_ref[0, r].astype(F32))
        plain += column_sum(da)
        if got is None:
            outs[0][r] = da.astype(BF16)
        else:
            da = da + got[r].astype(F32)
            outs[number][...] = da.astype(outs[number].dtype)
    sums[0:1] = weighted
    sums[1:2] = plain
    sums[2:8] = jnp.zeros((6, D), F32)


def normed_back(me, which, hops, grads, a, pieces, got=None):
    length = a.shape[1]
    rows = length // max(hops, 1)
    half = D // 2
    count = len(grads)
    if got is None:
        outs, out_specs = [sds(length, D)], [fixed(length, D)]
    elif hops:
        outs, out_specs = [sds(rows, D)] * hops, [fixed(rows, D)] * hops
    else:
        outs, out_specs = [sds(rows, D, dtype=F32)], [fixed(rows, D)]
    return call(
        functools.partial(normed_back_kernel, hops),
        outs + [sds(8, D, dtype=F32)],
        me, *grads, a, *pieces, *([] if got is None else [got]),
        grid=(1,),
        in_specs=[SCALARS]
        + [fixed(1, length, half)] * count
        + [pl.BlockSpec((1, length, D), lambda i: (which, 0, 0))]
        + [ANYWHERE] * 5
        + ([] if got is None else [fixed(length, D)]),
        out_specs=out_specs + [fixed(8, D)],
        scratch_shapes=[pltpu.VMEM((count, D, half), BF16), pltpu.SemaphoreType.DMA((count, 4))],
        flops=2 * count * length * half * D,
        moved=8 << 20,
        name="normed_back",
    )


def first_back_kernel(word, da_ref, got, x_ref, dx1, gain, dx_ref, low_ref):
    da = da_ref[...] + got[...].astype(F32)
    normal, inverse = normalize(x_ref[...].astype(F32))
    dx = dx1[...] + norm_back(da * gain[...], normal, inverse)
    dx_ref[...] = dx
    low_ref[...] = dx.astype(BF16)


def first_back(word, da, got, x, dx1, gain):
    rows = da.shape[0]
    return call(
        first_back_kernel,
        [sds(rows, D, dtype=F32), sds(rows, D)],
        word, da, got, x, dx1, gain,
        grid=(1,),
        in_specs=[SCALARS] + [fixed(rows, D)] * 4 + [fixed(1, D)],
        out_specs=[fixed(rows, D), fixed(rows, D)],
        moved=10 << 20,
        name="first_back",
    )


def unpack_down_kernel(core_ref, kept, got, out):
    core = core_ref[0]
    for half, source in ((core, kept), (1 - core, got)):
        for rh in range(2):
            for j in range(2):
                at = (rh * 2 + j) * 256
                rows = pl.ds(pl.multiple_of(half * 512 + rh * 256, 256), 256)
                out[0, rows, j * 512 : (j + 1) * 512] = source[at : at + 256].astype(F32)


def unpack_up_kernel(core_ref, kept_part, got, out_up, out_out):
    core = core_ref[0]
    for half, source in ((core, kept_part), (1 - core, got)):
        for j in range(4):
            at = (j // 2) * 640 + (j % 2) * 256
            columns = pl.ds(pl.multiple_of(j * 1024 + half * 512, 512), 512)
            out_up[0, :, columns] = source[at : at + 256].astype(F32)
        rows = pl.ds(pl.multiple_of(half * 128, 128), 128)
        for j in range(2):
            at = j * 640 + 512
            out_out[0, rows, j * 512 : (j + 1) * 512] = source[at : at + 128].astype(F32)


def unpack_qkv_kernel(core_ref, kept_part, got, out):
    core = core_ref[0]
    for half, source in ((core, kept_part), (1 - core, got)):
        for g in range(3):
            for f in range(4):
                columns = pl.ds(pl.multiple_of((g * 4 + f) * 256 + half * 128, 128), 128)
                out[0, :, columns] = source[
                    g * 256 : (g + 1) * 256, f * 128 : (f + 1) * 128
                ].astype(F32)


def unpack(kernel, core, pieces, shapes, name):
    return call(
        kernel,
        shapes,
        core, *pieces,
        in_specs=[SCALARS] + [INSIDE] * len(pieces),
        out_specs=jax.tree.map(lambda _: INSIDE, shapes),
        moved=10 << 20,
        name=name,
    )


def split_vector(values):
    pieces, offset = [], 0
    for length in (D, D, D, D, D, D, D, FF, D):
        pieces.append(values[offset : offset + length])
        offset += length
    return pieces


def shards(inputs, cotangent, segments, w_qkv, w_out, w_up, w_down, vectors):
    core = lax.axis_index("section")
    column = lax.axis_index("ctx")
    fs = lax.axis_index("fsdp")
    nf = lax.axis_size("fsdp")
    rows = inputs.shape[2]
    reach = (WIN - 1) // rows + 1
    halo = reach * rows
    first_core = core == 0
    me = fs.astype(jnp.int32).reshape(1)
    core_word = core.astype(jnp.int32).reshape(1)
    order = jnp.stack([fs ^ r for r in ROLL]).astype(jnp.int32)

    def pick(here, there):
        return jnp.where(first_core, here, there), jnp.where(first_core, there, here)

    mine = lambda values: lax.dynamic_index_in_dim(values, core, 0, keepdims=False)
    theirs = lambda values: lax.dynamic_index_in_dim(values, 1 - core, 0, keepdims=False)
    x_own, x_other = mine(inputs[:, 0]), theirs(inputs[:, 0])
    keep_a, send_a, keep_u, send_u, keep_d, send_d = pack_weights(
        tie(core_word, x_own), w_qkv, w_out, w_up, w_down
    )
    shard_a = pick(keep_a, swap(send_a))
    later = lambda value: tie(value, shard_a[0])

    shard_u = pick(keep_u, swap(later(send_u)))
    shard_d = pick(keep_d, swap(later(send_d)))
    both = tie(jnp.concatenate(pick(vectors, swap(vectors))), shard_u, shard_d)
    near = flip(both, "fsdp", 1)
    low_x = (fs & 1) == 0
    pair = jnp.concatenate([jnp.where(low_x, both, near), jnp.where(low_x, near, both)], 1)
    far = flip(pair, "fsdp", 2)
    low_y = (fs & 2) == 0
    packed = jnp.concatenate([jnp.where(low_y, pair, far), jnp.where(low_y, far, pair)], 1)
    packed = packed.astype(F32)

    a0 = Gather(shard_a[0])
    u0 = Gather(shard_u[0], a0.far)
    d0 = Gather(shard_d[0], a0.far)
    a1 = Gather(shard_a[1], d0.near)
    u1 = Gather(shard_u[1], a1.far)
    d1 = Gather(shard_d[1], a1.far)
    weights = ((a0, u0, d0), (a1, u1, d1))

    top = later(cotangent[:, 0])
    top_own, top_other = mine(top), theirs(top)
    marks = later(segments[:, 0])
    starts = jnp.stack([mine(marks), theirs(marks)])
    position = column * rows + jnp.arange(rows, dtype=jnp.int32)
    lo = jnp.maximum(starts, position[None] - (WIN - 1)) - (column * rows - halo)
    lo_column, lo = lo[:, :, None], lo[:, None, :]

    nought = later(jnp.zeros((), jnp.int32))
    key_index = lax.broadcasted_iota(jnp.int32, (halo + rows, LANES), 0) + nought
    lane = lax.broadcasted_iota(jnp.int32, (halo + rows, LANES), 1)
    placed = jnp.where(lane % 2 == 0, key_index // 256 * 256, key_index % 256)
    ek = jnp.where(lane < 6, placed, jnp.where(lane < 9, 1, 0)).astype(BF16)
    local_heads = HEADS // 2
    per_group = local_heads // nf
    local = jnp.arange(local_heads) + nought
    head = (local // per_group) * (2 * per_group) + core * per_group + local % per_group
    slopes = jnp.exp2(-0.5 * (head.astype(F32) + 1.0)) * (4.0 / WIN)
    first, second, third = [values.astype(F32) for values in split3(slopes)]
    eq = jnp.concatenate(
        [
            jnp.stack([first, first, second, second, third, third], 1),
            jnp.zeros((local_heads, LANES - 6), F32),
        ],
        1,
    ).reshape(local_heads // 2, 2, LANES)

    def start_halo(own, *after):
        pieces, block = [], own
        for hop in range(reach):
            block = step_along(tie(block, *after) if hop == 1 else block, "ctx", 1)
            pieces.append(block)
        return pieces

    def finish_return(first, hops, *after):
        carried, sent = first, first
        for hop, piece in enumerate(hops[1:]):
            sent = add_bf16(piece, tie(carried, *after) if hop == 0 else carried)
            carried = step_along(sent, "ctx", -1)
        return carried, sent

    def my_half(values, groups):
        view = values.reshape(groups, 2, -1)
        return jnp.where(first_core, view[:, 0], view[:, 1]).reshape(1, -1)

    def widen(values, groups):
        view = values.reshape(groups, 1, -1)
        zero = jnp.zeros_like(view)
        return jnp.where(
            first_core, jnp.concatenate([view, zero], 1), jnp.concatenate([zero, view], 1)
        ).reshape(-1)

    line = Line()
    run = line.run

    def forward(layer, x_own, x_other, first_hops):
        g1, b1, bq, bv, bo, g2, b2, bu, bd = [
            values.reshape(1, -1) for values in split_vector(packed[layer])
        ]
        bq, bv, bu = my_half(bq, nf), my_half(bv, nf), my_half(bu, nf)
        ga, gu, gd = weights[layer]
        wa, wu, wd = ga.pieces, gu.pieces, gd.pieces
        a_own, q, ko, vo = run(
            make_qkv, me, x_own, x_other, g1, b1, bq, bv, wa,
            after=(ek, eq, lo, lo_column, bu, first_hops if layer == 0 else ()),
        )
        earlier = ()
        for hop, block in enumerate(first_hops):
            block = tie(block, line.token if hop == 0 else ())
            earlier = run(
                make_kv, me, block, swap(block), reach, reach - 1 - hop, earlier, g1, b1, bv, wa,
                after=first_hops if hop == 0 else (),
            )
        a_halo, kh, vh = earlier
        o_other, e_other = run(
            attend, me, 1, q, kh, ko, vh, vo, lo_column, ek, eq, after=(gu.near,)
        )
        part = run(out_other, me, o_other, wa)
        o_own, e_own = run(
            attend, me, 0, q, kh, ko, vh, vo, lo_column, ek, eq, after=(gd.near,)
        )
        x1, h_own = run(
            middle, me, o_own, swap(part), x_own, bo, g2, b2, wa, after=(gu.far,)
        )
        o, e = (o_own, o_other), (e_own, e_other)
        h_other = swap(h_own)
        act_own, slope_own = run(up, me, h_own, bu, wu)
        act_other, slope_other = run(up, me, h_other, bu, wu)
        part = run(down_other, me, act_other, wd)
        y = run(last, me, act_own, swap(part), x1, bd, wd)
        stored = (
            x_own, a_own, a_halo, q, kh, ko, vh, vo, o, e, x1, h_own, h_other,
            act_own, slope_own, act_other, slope_other, g1, b1, g2,
        )
        return y, stored

    y0, stored0 = forward(0, x_own, x_other, start_halo(x_own, shard_a[0]))
    y0_other = swap(y0)
    y1, stored1 = forward(1, y0, y0_other, start_halo(y0, a1.near))
    y1_other = swap(y1)

    column_sums = Column()

    def step(block, *after):
        column_sums.step(block, line.token, *after)
        line.also += column_sums.sent

    def backward(layer, top_own, top_other, stored, before=()):
        last_layer = layer == 0
        (
            x_own, a_own, a_halo, q, kh, ko, vh, vo, o, e, x1, h_own, h_other,
            act_own, slope_own, act_other, slope_other, g1, b1, g2,
        ) = stored
        wa, wu, wd = (group.pieces for group in weights[layer])
        du_own, du_other, sums_up = run(
            act_back, me, top_own, top_other, slope_own, slope_other, wd
        )
        got = swap(run(up_back_other, me, du_other, wu))
        down_part = Scatter(*run(down_grad, order, act_own, act_other, top_own, top_other))
        if last_layer:
            before[1].third(line.token)
        dx1, db_own, sums_middle = run(middle_back, me, du_own, got, x1, top_own, g2, wu)
        db_other = swap(db_own)
        do = run(out_back, me, db_own, db_other, wa)
        up_part = Scatter(
            *run(up_grad, order, h_own, h_other, du_own, du_other, *o, db_own, db_other)
        )
        if last_layer:
            step(before[0].piece)

        def early(m):
            return run(attend_back, me, m, q, kh, ko, vh, vo, o[m], do, e[m], lo, ek)

        def own(m, start):
            return run(attend_back, me, m, q, kh, ko, vh, vo, o[m], do, e[m], lo, ek, start)

        begun_other, dkh_other, dvh_other = early(1)
        down_part.second(line.token)
        line.also += (down_part.half,)
        if last_layer:
            step(before[1].piece)
        part, sums_a = run(normed_back, me, 1, reach, (dkh_other, dvh_other), a_halo, wa)
        got = swap(part)
        begun_own, dkh_own, dvh_own = early(0)
        down_part.third(line.token)
        line.also = (down_part.piece,)
        *hops, sums_b = run(normed_back, me, 0, reach, (dkh_own, dvh_own), a_halo, wa, got)
        first = step_along(hops[0], "ctx", -1)
        carried = sent = first
        if last_layer:
            step(down_part.piece, hops)
        else:
            carried, sent = finish_return(first, hops)
        dq_other, dko_other, dvo_other = own(1, begun_other)
        part, sums_c = run(normed_back, me, 1, 0, (dq_other, dko_other, dvo_other), a_own, wa)
        got = swap(part)
        up_part.second(line.token)
        line.also += (up_part.half,)
        dq_own, dko_own, dvo_own = own(0, begun_own)
        *parts, sums_qkv = run(
            qkv_grad, order, a_own, a_halo, (dq_own, dq_other), (dko_own, dko_other),
            (dvo_own, dvo_other), (dkh_own, dkh_other), (dvh_own, dvh_other),
            after=(column_sums.outer_got, column_sums.inner_got) if last_layer else (sent,),
        )
        qkv_part = Scatter(*parts)
        up_part.third(line.token)
        line.also = (up_part.piece,)
        if last_layer:
            step(up_part.piece)
        da, sums_d = run(
            normed_back, me, 0, 0, (dq_own, dko_own, dvo_own), a_own, wa, got,
            after=() if last_layer else (carried,),
        )
        qkv_part.second(line.token)
        line.also += (qkv_part.half,)
        if last_layer:
            carried, sent = finish_return(first, hops, line.token)
            line.also += (sent,)
            qkv_part.third()
            step(qkv_part.piece)
        dx, dx_low = run(first_back, me, da, carried, x_own, dx1, g1)
        if not last_layer:
            step(down_part.piece)
        plain = sums_a[1] + sums_b[1] + sums_c[1] + sums_d[1]
        weighted = sums_a[0] + sums_b[0] + sums_c[0] + sums_d[0]
        vector = jnp.concatenate(
            [
                (weighted - b1[0] * plain) / g1[0], plain, widen(sums_qkv[0], nf),
                widen(sums_qkv[1], nf), sums_middle[2], sums_middle[0], sums_middle[1],
                widen(sums_up[0], nf), sums_middle[3],
            ]
        )
        return dx, dx_low, (up_part, qkv_part), vector

    _, dx1, parts1, vector1 = backward(1, top_own, top_other, stored1)
    dx1_other = swap(dx1)
    dx0, _, _, vector0 = backward(0, dx1, dx1_other, stored0, parts1)
    dx0_other = swap(dx0)
    stages = sums_over_all(jnp.stack([vector0, vector1]))
    step(None, stages[2])
    def by_micro(own, other):
        return jnp.where(first_core, jnp.stack([own, other]), jnp.stack([other, own]))

    activations = jnp.where(first_core, by_micro(y0, y0_other), by_micro(y1, y1_other))
    input_grad = jnp.where(
        first_core, by_micro(dx0, dx0_other), by_micro(dx1, dx1_other).astype(F32)
    )

    def exchange(first, second):
        kept, sent = pick(first, second)
        return kept, swap(sent)

    waiting = column_sums.outer_got, column_sums.inner_got
    waiting, activations, input_grad = lax.optimization_barrier((waiting, activations, input_grad))
    column_sums.outer_got, column_sums.inner_got = waiting
    step(None, stages[4])
    size = D // nf
    down1_sum, up1_sum, qkv1_sum, down0_sum, up0_sum, *_ = column_sums.sums
    grad_down = unpack(
        unpack_down_kernel, core_word, exchange(down0_sum, down1_sum),
        sds(1, FF // nf, D, dtype=F32), "unpack_down",
    )
    grad_up, grad_out = unpack(
        unpack_up_kernel, core_word, exchange(up0_sum, up1_sum),
        [sds(1, size, FF, dtype=F32), sds(1, size, D, dtype=F32)], "unpack_up",
    )
    waiting = column_sums.outer_got
    waiting, grad_down, grad_up, grad_out = lax.optimization_barrier(
        (waiting, grad_down, grad_up, grad_out)
    )
    column_sums.outer_got = waiting
    step(None, stages[-1])
    qkv0_sum = column_sums.sums[-1]
    grad_qkv = unpack(
        unpack_qkv_kernel, core_word, exchange(qkv0_sum, qkv1_sum),
        sds(1, size, 3 * D, dtype=F32), "unpack_qkv",
    )
    summed = stages[-1]
    length = summed.shape[1] // nf
    grad_vectors = lax.dynamic_slice(summed, (core, fs * length), (1, length))
    return (
        activations[None, :, None], input_grad[None, :, None],
        grad_qkv, grad_out, grad_up, grad_down, grad_vectors,
    )


def solution(mesh):
    placed = (
        P(None, "fsdp", "ctx", None),
        P(None, "fsdp", "ctx", None),
        P(None, "fsdp", "ctx"),
        P("section", "fsdp", None),
        P("section", "fsdp", None),
        P("section", "fsdp", None),
        P("section", "fsdp", None),
        P("section", "fsdp"),
    )
    return jax.shard_map(
        shards,
        mesh=mesh,
        in_specs=placed,
        out_specs=(
            P("section", None, "fsdp", "ctx", None),
            P("section", None, "fsdp", "ctx", None),
            P("section", "fsdp", None),
            P("section", "fsdp", None),
            P("section", "fsdp", None),
            P("section", "fsdp", None),
            P("section", "fsdp"),
        ),
        check_vma=False,
    )
```

profile of v0, /device:TPU:0, one launch (start us, length us, event | category | flops | bytes accessed | tf_op | source)
XLA Modules:
  0.0 797.6 jit_solution(10858703707865876336)
XLA Ops:
  3.9 5.9 collective-permute-start.6
  57.3 6.2 collective-permute-done.7.own_ref
  65.7 7.5 project_qkv.2
  77.8 7.1 project_earlier.4
  84.9 7.1 project_earlier.5
  92.1 7.7 collective-permute-done.14.w1
  101.3 13.2 %attention_forward.4 = (bf16[1,512,512]{2,1,0:T(8,128)(2,1)S(1)}, bf16[1,8,512,128]{3,2,1,0:T(8,128)(2,1)}) custom-call(s32[1]{0:T(128)} %bitcast.3.me_ref.word, bf16[2,512,512]{2,1,0:T(8,128)(2,1)} %get-tuple-element.285.q_ref, bf16[2,1024,512]{2,1,0:T(8,128)(2,1)} %get-tuple-element.286.kh_ref, bf16[2,512,512]{2,1,0:T(8,128)(2,1)} %get-tuple-element.287.ko_ref, ...), custom_call_target="tpu_custom_call" | custom-call | flops 5368709120 | bytes 6291456 | tf_op jit(solution)/shard_map/attention_forward/pallas_call | solution.py:144
  123.8 13.2 %attention_forward.5 = (bf16[1,512,512]{2,1,0:T(8,128)(2,1)S(1)}, bf16[1,8,512,128]{3,2,1,0:T(8,128)(2,1)}) custom-call(s32[1]{0:T(128)} %bitcast.3.me_ref.word, bf16[2,512,512]{2,1,0:T(8,128)(2,1)} %get-tuple-element.285.q_ref, bf16[2,1024,512]{2,1,0:T(8,128)(2,1)} %get-tuple-element.286.kh_ref, bf16[2,512,512]{2,1,0:T(8,128)(2,1)} %get-tuple-element.287.ko_ref, ...), custom_call_target="tpu_custom_call" | custom-call | flops 5368709120 | bytes 6291456 | tf_op jit(solution)/shard_map/attention_forward/pallas_call | solution.py:144
  143.6 6.7 up.6
  150.4 6.3 up.7
  172.0 14.4 %collective-permute-done.26.w1.refs_4_.refs_5_ = bf16[1024,512]{1,0:T(8,128)(2,1)S(1)} collective-permute-done((bf16[1024,512]{1,0:T(8,128)(2,1)S(1)}, bf16[1024,512]{1,0:T(8,128)(2,1)S(1)}, u32[]{:S(2)}, u32[]{:S(2)}) %collective-permute-start.26) | collective-permute-done | bytes 1048608 | tf_op jit(solution)/shard_map/ppermute | solution.py:29
  205.7 7.7 project_qkv.3
  213.5 6.6 collective-permute-done.31.own_ref
  224.2 7.0 project_earlier.6
  231.2 7.1 project_earlier.7
  238.3 7.8 collective-permute-done.34.w1
  247.1 13.2 %attention_forward.6 = (bf16[1,512,512]{2,1,0:T(8,128)(2,1)S(1)}, bf16[1,8,512,128]{3,2,1,0:T(8,128)(2,1)}) custom-call(s32[1]{0:T(128)} %bitcast.3.me_ref.word, bf16[2,512,512]{2,1,0:T(8,128)(2,1)} %get-tuple-element.317.q_ref, bf16[2,1024,512]{2,1,0:T(8,128)(2,1)} %get-tuple-element.318.kh_ref, bf16[2,512,512]{2,1,0:T(8,128)(2,1)} %get-tuple-element.319.ko_ref, ...), custom_call_target="tpu_custom_call" | custom-call | flops 5368709120 | bytes 6291456 | tf_op jit(solution)/shard_map/attention_forward/pallas_call | solution.py:144
  269.6 12.8 %attention_forward.7 = (bf16[1,512,512]{2,1,0:T(8,128)(2,1)S(1)}, bf16[1,8,512,128]{3,2,1,0:T(8,128)(2,1)}) custom-call(s32[1]{0:T(128)} %bitcast.3.me_ref.word, bf16[2,512,512]{2,1,0:T(8,128)(2,1)} %get-tuple-element.317.q_ref, bf16[2,1024,512]{2,1,0:T(8,128)(2,1)} %get-tuple-element.318.kh_ref, bf16[2,512,512]{2,1,0:T(8,128)(2,1)} %get-tuple-element.319.ko_ref, ...), custom_call_target="tpu_custom_call" | custom-call | flops 5368709120 | bytes 6291456 | tf_op jit(solution)/shard_map/attention_forward/pallas_call | solution.py:144
  289.3 6.7 up.8
  296.0 6.3 up.9
  313.7 7.8 act_back.2
  329.6 9.3 %down_grad.2 = (bf16[2,512,512]{2,1,0:T(8,128)(2,1)}, bf16[2,512,512]{2,1,0:T(8,128)(2,1)}, bf16[2,512,512]{2,1,0:T(8,128)(2,1)}, bf16[2,512,512]{2,1,0:T(8,128)(2,1)}) custom-call(s32[4]{0:T(128)S(1)} %pad_add_fusion.order, bf16[512,2048]{1,0:T(8,128)(2,1)} %copy-done.48, bf16[512,2048]{1,0:T(8,128)(2,1)} %copy-done.107, bf16[512,1024]{1,0:T(8,128)(2,1)S(1)} %copy-done.26, ...), custom_call_target="tpu_custom_call" | custom-call | flops 4294967296 | bytes 10485760 | tf_op jit(solution)/shard_map/down_grad/pallas_call | solution.py:144
  339.1 6.0 middle_back.2
  351.0 9.8 %up_grad.2 = (bf16[2,640,512]{2,1,0:T(8,128)(2,1)}, bf16[2,640,512]{2,1,0:T(8,128)(2,1)}, bf16[2,640,512]{2,1,0:T(8,128)(2,1)}, bf16[2,640,512]{2,1,0:T(8,128)(2,1)}) custom-call(s32[4]{0:T(128)S(1)} %pad_add_fusion.order, bf16[512,1024]{1,0:T(8,128)(2,1)S(1)} %copy-done.101, bf16[512,1024]{1,0:T(8,128)(2,1)S(1)} %copy-done.103, ...), custom_call_target="tpu_custom_call" | custom-call | flops 5368709120 | bytes 14680064 | tf_op jit(solution)/shard_map/up_grad/pallas_call | solution.py:144
  360.8 12.4 %attention_backward.8 = (f32[1,512,512]{2,1,0:T(8,128)S(1)}, bf16[1,1024,512]{2,1,0:T(8,128)(2,1)S(1)}, bf16[1,1024,512]{2,1,0:T(8,128)(2,1)S(1)}) custom-call(s32[1]{0:T(128)} %bitcast.3.me_ref.word, bf16[2,512,512]{2,1,0:T(8,128)(2,1)} %get-tuple-element.317.q_ref, bf16[2,1024,512]{2,1,0:T(8,128)(2,1)} %get-tuple-element.318.kh_ref, ...), custom_call_target="tpu_custom_call" | custom-call | flops 8053062656 | bytes 8388608 | tf_op jit(solution)/shard_map/attention_backward/pallas_call | solution.py:144
  383.0 12.3 %attention_backward.9 = (f32[1,512,512]{2,1,0:T(8,128)S(1)}, bf16[1,1024,512]{2,1,0:T(8,128)(2,1)S(1)}, bf16[1,1024,512]{2,1,0:T(8,128)(2,1)S(1)}) custom-call(s32[1]{0:T(128)} %bitcast.3.me_ref.word, bf16[2,512,512]{2,1,0:T(8,128)(2,1)} %get-tuple-element.317.q_ref, bf16[2,1024,512]{2,1,0:T(8,128)(2,1)} %get-tuple-element.318.kh_ref, ...), custom_call_target="tpu_custom_call" | custom-call | flops 8053062656 | bytes 8388608 | tf_op jit(solution)/shard_map/attention_backward/pallas_call | solution.py:144
  403.0 7.8 attention_backward.10
  414.1 7.2 collective-permute-done.52
  424.2 7.8 attention_backward.11
  433.7 12.4 %qkv_grad.2 = (bf16[2,384,512]{2,1,0:T(8,128)(2,1)}, bf16[2,384,512]{2,1,0:T(8,128)(2,1)}, bf16[2,384,512]{2,1,0:T(8,128)(2,1)}, bf16[2,384,512]{2,1,0:T(8,128)(2,1)}, f32[8,512]{1,0:T(8,128)S(1)}) custom-call(s32[4]{0:T(128)S(1)} %pad_add_fusion.order, bf16[2,512,1024]{2,1,0:T(8,128)(2,1)S(1)} %copy-done.15, bf16[2,1024,1024]{2,1,0:T(8,128)(2,1)S(1)} %copy-done.9, ...), custom_call_target="tpu_custom_call" | custom-call | flops 7516192768 | bytes 16777216 | tf_op jit(solution)/shard_map/qkv_grad/pallas_call | solution.py:144
  450.4 10.2 %collective-permute-done.57.got = bf16[512,1024]{1,0:T(8,128)(2,1)S(1)} collective-permute-done((bf16[512,1024]{1,0:T(8,128)(2,1)S(1)}, bf16[512,1024]{1,0:T(8,128)(2,1)S(1)}, u32[]{:S(2)}, u32[]{:S(2)}) %collective-permute-start.57) | collective-permute-done | bytes 1048608 | tf_op jit(solution)/shard_map/ppermute | solution.py:35
  483.5 8.2 %act_back.3 = (bf16[512,2048]{1,0:T(8,128)(2,1)S(1)}, bf16[512,2048]{1,0:T(8,128)(2,1)S(1)}, f32[8,2048]{1,0:T(8,128)S(1)}) custom-call(s32[1]{0:T(128)} %bitcast.3.me_ref.word, bf16[512,1024]{1,0:T(8,128)(2,1)S(1)} %copy-done.29, bf16[512,1024]{1,0:T(8,128)(2,1)} %collective-permute-done.62.other, bf16[512,2048]{1,0:T(8,128)(2,1)} %get-tuple-element.404.slope_own, ...), custom_call_target="tpu_custom_call" | custom-call | flops 4294967296 | bytes 16777216 | tf_op jit(solution)/shard_map/act_back/pallas_call | solution.py:144
  502.0 9.7 %down_grad.3 = (bf16[2,512,512]{2,1,0:T(8,128)(2,1)}, bf16[2,512,512]{2,1,0:T(8,128)(2,1)}, bf16[2,512,512]{2,1,0:T(8,128)(2,1)}, bf16[2,512,512]{2,1,0:T(8,128)(2,1)}) custom-call(s32[4]{0:T(128)S(1)} %copy-done.95, bf16[512,2048]{1,0:T(8,128)(2,1)} %copy-done.45, bf16[512,2048]{1,0:T(8,128)(2,1)} %copy-done.104, bf16[512,1024]{1,0:T(8,128)(2,1)S(1)} %copy-done.30, ...), custom_call_target="tpu_custom_call" | custom-call | flops 4294967296 | bytes 10485760 | tf_op jit(solution)/shard_map/down_grad/pallas_call | solution.py:144
  522.0 9.8 %up_grad.3 = (bf16[2,640,512]{2,1,0:T(8,128)(2,1)}, bf16[2,640,512]{2,1,0:T(8,128)(2,1)}, bf16[2,640,512]{2,1,0:T(8,128)(2,1)}, bf16[2,640,512]{2,1,0:T(8,128)(2,1)}) custom-call(s32[4]{0:T(128)S(1)} %copy-done.95, bf16[512,1024]{1,0:T(8,128)(2,1)S(1)} %copy-done.97, bf16[512,1024]{1,0:T(8,128)(2,1)S(1)} %copy-done.99, ...), custom_call_target="tpu_custom_call" | custom-call | flops 5368709120 | bytes 14680064 | tf_op jit(solution)/shard_map/up_grad/pallas_call | solution.py:144
  533.0 12.4 %attention_backward.12 = (f32[1,512,512]{2,1,0:T(8,128)S(1)}, bf16[1,1024,512]{2,1,0:T(8,128)(2,1)S(1)}, bf16[1,1024,512]{2,1,0:T(8,128)(2,1)S(1)}) custom-call(s32[1]{0:T(128)} %bitcast.3.me_ref.word, bf16[2,512,512]{2,1,0:T(8,128)(2,1)} %get-tuple-element.285.q_ref, bf16[2,1024,512]{2,1,0:T(8,128)(2,1)} %get-tuple-element.286.kh_ref, ...), custom_call_target="tpu_custom_call" | custom-call | flops 8053062656 | bytes 8388608 | tf_op jit(solution)/shard_map/attention_backward/pallas_call | solution.py:144
  546.8 15.7 %collective-permute-done.65 = bf16[1280,512]{1,0:T(8,128)(2,1)S(1)} collective-permute-done((bf16[1280,512]{1,0:T(8,128)(2,1)S(1)}, bf16[1280,512]{1,0:T(8,128)(2,1)S(1)}, u32[]{:S(2)}, u32[]{:S(2)}) %collective-permute-start.65) | collective-permute-done | bytes 1310752 | tf_op jit(solution)/shard_map/ppermute | solution.py:29
  575.9 12.5 %attention_backward.13 = (f32[1,512,512]{2,1,0:T(8,128)S(1)}, bf16[1,1024,512]{2,1,0:T(8,128)(2,1)S(1)}, bf16[1,1024,512]{2,1,0:T(8,128)(2,1)S(1)}) custom-call(s32[1]{0:T(128)} %bitcast.3.me_ref.word, bf16[2,512,512]{2,1,0:T(8,128)(2,1)} %get-tuple-element.285.q_ref, bf16[2,1024,512]{2,1,0:T(8,128)(2,1)} %get-tuple-element.286.kh_ref, ...), custom_call_target="tpu_custom_call" | custom-call | flops 8053062656 | bytes 8388608 | tf_op jit(solution)/shard_map/attention_backward/pallas_call | solution.py:144
  601.4 8.7 %collective-permute-start.76 = (bf16[1280,512]{1,0:T(8,128)(2,1)}, bf16[1280,512]{1,0:T(8,128)(2,1)S(1)}, u32[]{:S(2)}, u32[]{:S(2)}) collective-permute-start(bf16[1280,512]{1,0:T(8,128)(2,1)} %pad_select_fusion.1), channel_id=1, source_target_pairs={{0,4},{4,0},{8,12},{12,8},{1,5},{5,1},{9,13},{13,9},{2,6},{6,2},{1... | collective-permute-start | bytes 3932168 | tf_op jit(solution)/shard_map/ppermute | solution.py:29
  610.2 7.8 attention_backward.14
  629.3 7.8 attention_backward.15
  639.5 12.5 %qkv_grad.3 = (bf16[2,384,512]{2,1,0:T(8,128)(2,1)}, bf16[2,384,512]{2,1,0:T(8,128)(2,1)}, bf16[2,384,512]{2,1,0:T(8,128)(2,1)}, bf16[2,384,512]{2,1,0:T(8,128)(2,1)}, f32[8,512]{1,0:T(8,128)S(1)}) custom-call(s32[4]{0:T(128)S(1)} %copy-done.95, bf16[2,512,1024]{2,1,0:T(8,128)(2,1)S(1)} %copy-done.14, bf16[2,1024,1024]{2,1,0:T(8,128)(2,1)S(1)} %copy-done.8, ...), custom_call_target="tpu_custom_call" | custom-call | flops 7516192768 | bytes 16777216 | tf_op jit(solution)/shard_map/qkv_grad/pallas_call | solution.py:144
  671.2 8.2 %collective-permute-done.85 = bf16[2,384,512]{2,1,0:T(8,128)(2,1)S(1)} collective-permute-done((bf16[2,384,512]{2,1,0:T(8,128)(2,1)S(1)}, bf16[2,384,512]{2,1,0:T(8,128)(2,1)S(1)}, u32[]{:S(2)}, u32[]{:S(2)}) %collective-permute-start.85) | collective-permute-done | bytes 786464 | tf_op jit(solution)/shard_map/ppermute | solution.py:29
  681.8 7.0 collective-permute-done.88
  691.8 5.7 collective-permute-done.82
  701.8 18.2 %collective-permute-done.92.got = bf16[512,1024]{1,0:T(8,128)(2,1)S(1)} collective-permute-done((bf16[512,1024]{1,0:T(8,128)(2,1)S(1)}, bf16[512,1024]{1,0:T(8,128)(2,1)S(1)}, u32[]{:S(2)}, u32[]{:S(2)}) %collective-permute-start.92) | collective-permute-done | bytes 1048608 | tf_op jit(solution)/shard_map/ppermute | solution.py:35
  729.2 10.8 %collective-permute-done.89 = bf16[1024,512]{1,0:T(8,128)(2,1)S(1)} collective-permute-done((bf16[1024,512]{1,0:T(8,128)(2,1)S(1)}, bf16[1024,512]{1,0:T(8,128)(2,1)S(1)}, u32[]{:S(2)}, u32[]{:S(2)}) %collective-permute-start.89) | collective-permute-done | bytes 1048608 | tf_op jit(solution)/shard_map/ppermute | solution.py:29
  754.9 16.4 %collective-permute-done.95 = bf16[1280,512]{1,0:T(8,128)(2,1)S(1)} collective-permute-done((bf16[1280,512]{1,0:T(8,128)(2,1)S(1)}, bf16[1280,512]{1,0:T(8,128)(2,1)S(1)}, u32[]{:S(2)}, u32[]{:S(2)}) %collective-permute-start.95) | collective-permute-done | bytes 1310752 | tf_op jit(solution)/shard_map/ppermute | solution.py:29
  779.1 13.6 %collective-permute-done.101 = bf16[768,512]{1,0:T(8,128)(2,1)S(1)} collective-permute-done((bf16[768,512]{1,0:T(8,128)(2,1)S(1)}, bf16[768,512]{1,0:T(8,128)(2,1)S(1)}, u32[]{:S(2)}, u32[]{:S(2)}) %collective-permute-start.101) | collective-permute-done | bytes 786464 | tf_op jit(solution)/shard_map/ppermute | solution.py:29
  (690 shorter events, 335.1 us)
Async XLA Ops:
  3.9 34.4 %collective-permute-start.6 = (bf16[512,1024]{1,0:T(8,128)(2,1)}, bf16[512,1024]{1,0:T(8,128)(2,1)}, u32[]{:S(2)}, u32[]{:S(2)}) collective-permute-start(bf16[512,1024]{1,0:T(8,128)(2,1)} %get-tuple-element.564.own_ref.x_ref), channel_id=1, source_target_pairs={{0,4},{4,8},{8,12},{1,5},{5,9},{9,13},{2,6},{6,10},{10,14},{3,7},{... | collective-permute-start | bytes 3145736 | tf_op jit(solution)/shard_map/ppermute | solution.py:35
  19.6 28.7 %collective-permute-start.8 = (bf16[1024,512]{1,0:T(8,128)(2,1)S(1)}, bf16[1024,512]{1,0:T(8,128)(2,1)S(1)}, u32[]{:S(2)}, u32[]{:S(2)}) collective-permute-start(bf16[1024,512]{1,0:T(8,128)(2,1)S(1)} %get-tuple-element.562.w0.refs_3_.refs_4_), channel_id=1, source_target_pairs={{0,1},{1,0},{2,3},{3,2},{4,5},{5,4},{6,7},{7,6},{8,9},{9,8},{10,11... | collective-permute-start | bytes 3145736 | tf_op jit(solution)/shard_map/ppermute | solution.py:29
  21.1 28.5 %collective-permute-start.9 = (bf16[1024,512]{1,0:T(8,128)(2,1)S(1)}, bf16[1024,512]{1,0:T(8,128)(2,1)}, u32[]{:S(2)}, u32[]{:S(2)}) collective-permute-start(bf16[1024,512]{1,0:T(8,128)(2,1)S(1)} %get-tuple-element.562.w0.refs_3_.refs_4_), channel_id=1, source_target_pairs={{0,2},{1,3},{2,0},{3,1},{4,6},{5,7},{6,4},{7,5},{8,10},{9,11},{10,... | collective-permute-start | bytes 3145736 | tf_op jit(solution)/shard_map/ppermute | solution.py:29
  38.3 25.2 %collective-permute-start.7 = (bf16[512,1024]{1,0:T(8,128)(2,1)}, bf16[512,1024]{1,0:T(8,128)(2,1)}, u32[]{:S(2)}, u32[]{:S(2)}) collective-permute-start(bf16[512,1024]{1,0:T(8,128)(2,1)} %collective-permute-done.6.own_ref), channel_id=1, source_target_pairs={{0,4},{4,8},{8,12},{1,5},{5,9},{9,13},{2,6},{6,10},{10,14},{3,7},{... | collective-permute-start | bytes 3145736 | tf_op jit(solution)/shard_map/ppermute | solution.py:35
  73.8 26.0 %collective-permute-start.14 = (bf16[1024,512]{1,0:T(8,128)(2,1)S(1)}, bf16[1024,512]{1,0:T(8,128)(2,1)S(1)}, u32[]{:S(2)}, u32[]{:S(2)}) collective-permute-start(bf16[1024,512]{1,0:T(8,128)(2,1)S(1)} %copy-done.18), channel_id=1, source_target_pairs={{0,1},{1,0},{2,3},{3,2},{4,5},{5,4},{6,7},{7,6},{8,9},{9,8},{10,11... | collective-permute-start | bytes 3145736 | tf_op jit(solution)/shard_map/ppermute | solution.py:29
  75.3 26.1 %collective-permute-start.15 = (bf16[1024,512]{1,0:T(8,128)(2,1)S(1)}, bf16[1024,512]{1,0:T(8,128)(2,1)S(1)}, u32[]{:S(2)}, u32[]{:S(2)}) collective-permute-start(bf16[1024,512]{1,0:T(8,128)(2,1)S(1)} %copy-done.18), channel_id=1, source_target_pairs={{0,2},{1,3},{2,0},{3,1},{4,6},{5,7},{6,4},{7,5},{8,10},{9,11},{10,... | collective-permute-start | bytes 3145736 | tf_op jit(solution)/shard_map/ppermute | solution.py:29
  76.8 44.7 %collective-permute-start.16 = (bf16[1024,512]{1,0:T(8,128)(2,1)S(1)}, bf16[1024,512]{1,0:T(8,128)(2,1)S(1)}, u32[]{:S(2)}, u32[]{:S(2)}) collective-permute-start(bf16[1024,512]{1,0:T(8,128)(2,1)S(1)} %copy-done.20), channel_id=1, source_target_pairs={{0,1},{1,0},{2,3},{3,2},{4,5},{5,4},{6,7},{7,6},{8,9},{9,8},{10,11... | collective-permute-start | bytes 3145736 | tf_op jit(solution)/shard_map/ppermute | solution.py:29
  77.3 46.5 %collective-permute-start.17 = (bf16[1024,512]{1,0:T(8,128)(2,1)S(1)}, bf16[1024,512]{1,0:T(8,128)(2,1)S(1)}, u32[]{:S(2)}, u32[]{:S(2)}) collective-permute-start(bf16[1024,512]{1,0:T(8,128)(2,1)S(1)} %copy-done.20), channel_id=1, source_target_pairs={{0,2},{1,3},{2,0},{3,1},{4,6},{5,7},{6,4},{7,5},{8,10},{9,11},{10,... | collective-permute-start | bytes 3145736 | tf_op jit(solution)/shard_map/ppermute | solution.py:29
  160.9 25.5 %collective-permute-start.26 = (bf16[1024,512]{1,0:T(8,128)(2,1)S(1)}, bf16[1024,512]{1,0:T(8,128)(2,1)S(1)}, u32[]{:S(2)}, u32[]{:S(2)}) collective-permute-start(bf16[1024,512]{1,0:T(8,128)(2,1)S(1)} %get-tuple-element.305.w0.refs_3_.refs_4_), channel_id=1, source_target_pairs={{0,1},{1,0},{2,3},{3,2},{4,5},{5,4},{6,7},{7,6},{8,9},{9,8},{10,11... | collective-permute-start | bytes 3145736 | tf_op jit(solution)/shard_map/ppermute | solution.py:29
  162.0 25.9 %collective-permute-start.27 = (bf16[1024,512]{1,0:T(8,128)(2,1)S(1)}, bf16[1024,512]{1,0:T(8,128)(2,1)S(1)}, u32[]{:S(2)}, u32[]{:S(2)}) collective-permute-start(bf16[1024,512]{1,0:T(8,128)(2,1)S(1)} %get-tuple-element.305.w0.refs_3_.refs_4_), channel_id=1, source_target_pairs={{0,2},{1,3},{2,0},{3,1},{4,6},{5,7},{6,4},{7,5},{8,10},{9,11},{10,... | collective-permute-start | bytes 3145736 | tf_op jit(solution)/shard_map/ppermute | solution.py:29
  167.2 26.6 %collective-permute-start.30 = (bf16[512,1024]{1,0:T(8,128)(2,1)}, bf16[512,1024]{1,0:T(8,128)(2,1)}, u32[]{:S(2)}, u32[]{:S(2)}) collective-permute-start(bf16[512,1024]{1,0:T(8,128)(2,1)} %down_own.2.own_ref.x_ref), channel_id=1, source_target_pairs={{0,4},{4,8},{8,12},{1,5},{5,9},{9,13},{2,6},{6,10},{10,14},{3,7},{... | collective-permute-start | bytes 3145736 | tf_op jit(solution)/shard_map/ppermute | solution.py:35
  172.0 30.6 %collective-permute-start.25 = (bf16[512,1024]{1,0:T(8,128)(2,1)}, bf16[512,1024]{1,0:T(8,128)(2,1)}, u32[]{:S(2)}, u32[]{:S(2)}) collective-permute-start(bf16[512,1024]{1,0:T(8,128)(2,1)} %down_own.2.own_ref.x_ref), channel_id=1, source_target_pairs={{0,16},{16,0},{1,17},{17,1},{2,18},{18,2},{3,19},{19,3},{4,20},{20... | collective-permute-start | bytes 3145736 | tf_op jit(solution)/shard_map/ppermute | solution.py:29
  193.8 26.3 %collective-permute-start.31 = (bf16[512,1024]{1,0:T(8,128)(2,1)}, bf16[512,1024]{1,0:T(8,128)(2,1)}, u32[]{:S(2)}, u32[]{:S(2)}) collective-permute-start(bf16[512,1024]{1,0:T(8,128)(2,1)} %collective-permute-done.30.own_ref), channel_id=1, source_target_pairs={{0,4},{4,8},{8,12},{1,5},{5,9},{9,13},{2,6},{6,10},{10,14},{3,7},{... | collective-permute-start | bytes 3145736 | tf_op jit(solution)/shard_map/ppermute | solution.py:35
  220.1 26.0 %collective-permute-start.34 = (bf16[1024,512]{1,0:T(8,128)(2,1)S(1)}, bf16[1024,512]{1,0:T(8,128)(2,1)S(1)}, u32[]{:S(2)}, u32[]{:S(2)}) collective-permute-start(bf16[1024,512]{1,0:T(8,128)(2,1)S(1)} %copy-done.22), channel_id=1, source_target_pairs={{0,1},{1,0},{2,3},{3,2},{4,5},{5,4},{6,7},{7,6},{8,9},{9,8},{10,11... | collective-permute-start | bytes 3145736 | tf_op jit(solution)/shard_map/ppermute | solution.py:29
  221.1 26.0 %collective-permute-start.35 = (bf16[1024,512]{1,0:T(8,128)(2,1)S(1)}, bf16[1024,512]{1,0:T(8,128)(2,1)S(1)}, u32[]{:S(2)}, u32[]{:S(2)}) collective-permute-start(bf16[1024,512]{1,0:T(8,128)(2,1)S(1)} %copy-done.22), channel_id=1, source_target_pairs={{0,2},{1,3},{2,0},{3,1},{4,6},{5,7},{6,4},{7,5},{8,10},{9,11},{10,... | collective-permute-start | bytes 3145736 | tf_op jit(solution)/shard_map/ppermute | solution.py:29
  222.6 46.0 %collective-permute-start.36 = (bf16[1024,512]{1,0:T(8,128)(2,1)S(1)}, bf16[1024,512]{1,0:T(8,128)(2,1)S(1)}, u32[]{:S(2)}, u32[]{:S(2)}) collective-permute-start(bf16[1024,512]{1,0:T(8,128)(2,1)S(1)} %copy-done.24), channel_id=1, source_target_pairs={{0,1},{1,0},{2,3},{3,2},{4,5},{5,4},{6,7},{7,6},{8,9},{9,8},{10,11... | collective-permute-start | bytes 3145736 | tf_op jit(solution)/shard_map/ppermute | solution.py:29
  223.5 46.0 %collective-permute-start.37 = (bf16[1024,512]{1,0:T(8,128)(2,1)S(1)}, bf16[1024,512]{1,0:T(8,128)(2,1)S(1)}, u32[]{:S(2)}, u32[]{:S(2)}) collective-permute-start(bf16[1024,512]{1,0:T(8,128)(2,1)S(1)} %copy-done.24), channel_id=1, source_target_pairs={{0,2},{1,3},{2,0},{3,1},{4,6},{5,7},{6,4},{7,5},{8,10},{9,11},{10,... | collective-permute-start | bytes 3145736 | tf_op jit(solution)/shard_map/ppermute | solution.py:29
  345.6 27.7 %collective-permute-start.45 = (bf16[2,512,512]{2,1,0:T(8,128)(2,1)S(1)}, bf16[2,512,512]{2,1,0:T(8,128)(2,1)S(1)}, u32[]{:S(2)}, u32[]{:S(2)}) collective-permute-start(bf16[2,512,512]{2,1,0:T(8,128)(2,1)S(1)} %copy-done.158), channel_id=1, source_target_pairs={{0,1},{1,0},{2,3},{3,2},{4,5},{5,4},{6,7},{7,6},{8,9},{9,8},{10,11... | collective-permute-start | bytes 3145736 | tf_op jit(solution)/shard_map/ppermute | solution.py:29
  346.7 26.6 %collective-permute-start.46 = (bf16[2,512,512]{2,1,0:T(8,128)(2,1)S(1)}, bf16[2,512,512]{2,1,0:T(8,128)(2,1)S(1)}, u32[]{:S(2)}, u32[]{:S(2)}) collective-permute-start(bf16[2,512,512]{2,1,0:T(8,128)(2,1)S(1)} %copy-done.157), channel_id=1, source_target_pairs={{0,2},{1,3},{2,0},{3,1},{4,6},{5,7},{6,4},{7,5},{8,10},{9,11},{10,... | collective-permute-start | bytes 3145736 | tf_op jit(solution)/shard_map/ppermute | solution.py:29
  380.9 40.4 %collective-permute-start.52 = (bf16[2,640,512]{2,1,0:T(8,128)(2,1)}, bf16[2,640,512]{2,1,0:T(8,128)(2,1)S(1)}, u32[]{:S(2)}, u32[]{:S(2)}) collective-permute-start(bf16[2,640,512]{2,1,0:T(8,128)(2,1)} %get-tuple-element.352), channel_id=1, source_target_pairs={{0,1},{1,0},{2,3},{3,2},{4,5},{5,4},{6,7},{7,6},{8,9},{9,8},{10,11... | collective-permute-start | bytes 3932168 | tf_op jit(solution)/shard_map/ppermute | solution.py:29
  382.0 40.2 %collective-permute-start.53 = (bf16[2,640,512]{2,1,0:T(8,128)(2,1)}, bf16[2,640,512]{2,1,0:T(8,128)(2,1)S(1)}, u32[]{:S(2)}, u32[]{:S(2)}) collective-permute-start(bf16[2,640,512]{2,1,0:T(8,128)(2,1)} %get-tuple-element.379), channel_id=1, source_target_pairs={{0,2},{1,3},{2,0},{3,1},{4,6},{5,7},{6,4},{7,5},{8,10},{9,11},{10,... | collective-permute-start | bytes 3932168 | tf_op jit(solution)/shard_map/ppermute | solution.py:29
  401.6 30.4 %collective-permute-start.54 = (bf16[512,1024]{1,0:T(8,128)(2,1)S(1)}, bf16[512,1024]{1,0:T(8,128)(2,1)S(1)}, u32[]{:S(2)}, u32[]{:S(2)}) collective-permute-start(bf16[512,1024]{1,0:T(8,128)(2,1)S(1)} %get-tuple-element.371), channel_id=1, source_target_pairs={{4,0},{8,4},{12,8},{5,1},{9,5},{13,9},{6,2},{10,6},{14,10},{7,3},{... | collective-permute-start | bytes 3145736 | tf_op jit(solution)/shard_map/ppermute | solution.py:35
  422.3 24.8 %collective-permute-start.56 = (bf16[640,512]{1,0:T(8,128)(2,1)S(1)}, bf16[640,512]{1,0:T(8,128)(2,1)S(1)}, u32[]{:S(2)}, u32[]{:S(2)}) collective-permute-start(bf16[640,512]{1,0:T(8,128)(2,1)S(1)} %fusion.15), channel_id=1, source_target_pairs={{0,1},{1,0},{2,3},{3,2},{4,5},{5,4},{6,7},{7,6},{8,9},{9,8},{10,11... | collective-permute-start | bytes 1966088 | tf_op jit(solution)/shard_map/ppermute | solution.py:29
  424.2 36.5 %collective-permute-start.58 = (bf16[512,1024]{1,0:T(8,128)(2,1)S(1)}, bf16[512,1024]{1,0:T(8,128)(2,1)S(1)}, u32[]{:S(2)}, u32[]{:S(2)}) collective-permute-start(bf16[512,1024]{1,0:T(8,128)(2,1)S(1)} %get-tuple-element.377), channel_id=1, source_target_pairs={{0,16},{16,0},{1,17},{17,1},{2,18},{18,2},{3,19},{19,3},{4,20},{20... | collective-permute-start | bytes 3145736 | tf_op jit(solution)/shard_map/ppermute | solution.py:29
  432.4 28.2 %collective-permute-start.57 = (bf16[512,1024]{1,0:T(8,128)(2,1)S(1)}, bf16[512,1024]{1,0:T(8,128)(2,1)S(1)}, u32[]{:S(2)}, u32[]{:S(2)}) collective-permute-start(bf16[512,1024]{1,0:T(8,128)(2,1)S(1)} %add_convert_fusion.9), channel_id=1, source_target_pairs={{4,0},{8,4},{12,8},{5,1},{9,5},{13,9},{6,2},{10,6},{14,10},{7,3},{... | collective-permute-start | bytes 3145736 | tf_op jit(solution)/shard_map/ppermute | solution.py:35
  495.3 36.5 %collective-permute-start.61 = (bf16[1024,512]{1,0:T(8,128)(2,1)S(1)}, bf16[1024,512]{1,0:T(8,128)(2,1)S(1)}, u32[]{:S(2)}, u32[]{:S(2)}) collective-permute-start(bf16[1024,512]{1,0:T(8,128)(2,1)S(1)} %copy-done.109), channel_id=1, source_target_pairs={{0,4},{4,0},{8,12},{12,8},{1,5},{5,1},{9,13},{13,9},{2,6},{6,2},{1... | collective-permute-start | bytes 3145736 | tf_op jit(solution)/shard_map/ppermute | solution.py:29
  516.6 28.9 %collective-permute-start.71 = (bf16[2,512,512]{2,1,0:T(8,128)(2,1)S(1)}, bf16[2,512,512]{2,1,0:T(8,128)(2,1)S(1)}, u32[]{:S(2)}, u32[]{:S(2)}) collective-permute-start(bf16[2,512,512]{2,1,0:T(8,128)(2,1)S(1)} %copy-done.156), channel_id=1, source_target_pairs={{0,1},{1,0},{2,3},{3,2},{4,5},{5,4},{6,7},{7,6},{8,9},{9,8},{10,11... | collective-permute-start | bytes 3145736 | tf_op jit(solution)/shard_map/ppermute | solution.py:29
  517.7 27.7 %collective-permute-start.72 = (bf16[2,512,512]{2,1,0:T(8,128)(2,1)S(1)}, bf16[2,512,512]{2,1,0:T(8,128)(2,1)S(1)}, u32[]{:S(2)}, u32[]{:S(2)}) collective-permute-start(bf16[2,512,512]{2,1,0:T(8,128)(2,1)S(1)} %copy-done.155), channel_id=1, source_target_pairs={{0,2},{1,3},{2,0},{3,1},{4,6},{5,7},{6,4},{7,5},{8,10},{9,11},{10,... | collective-permute-start | bytes 3145736 | tf_op jit(solution)/shard_map/ppermute | solution.py:29
  531.8 30.7 %collective-permute-start.65 = (bf16[1280,512]{1,0:T(8,128)(2,1)S(1)}, bf16[1280,512]{1,0:T(8,128)(2,1)S(1)}, u32[]{:S(2)}, u32[]{:S(2)}) collective-permute-start(bf16[1280,512]{1,0:T(8,128)(2,1)S(1)} %copy-done.108), channel_id=1, source_target_pairs={{0,4},{4,0},{8,12},{12,8},{1,5},{5,1},{9,13},{13,9},{2,6},{6,2},{1... | collective-permute-start | bytes 3932168 | tf_op jit(solution)/shard_map/ppermute | solution.py:29
  570.6 28.3 %collective-permute-start.70 = (bf16[1280,512]{1,0:T(8,128)(2,1)S(1)}, bf16[1280,512]{1,0:T(8,128)(2,1)S(1)}, u32[]{:S(2)}, u32[]{:S(2)}) collective-permute-start(bf16[1280,512]{1,0:T(8,128)(2,1)S(1)} %add_convert_fusion.3), channel_id=1, source_target_pairs={{4,8},{8,4},{5,9},{9,5},{6,10},{10,6},{7,11},{11,7},{20,24},{24,20... | collective-permute-start | bytes 3932168 | tf_op jit(solution)/shard_map/ppermute | solution.py:112
  571.3 27.6 %collective-permute-start.69 = (bf16[1024,512]{1,0:T(8,128)(2,1)S(1)}, bf16[1024,512]{1,0:T(8,128)(2,1)S(1)}, u32[]{:S(2)}, u32[]{:S(2)}) collective-permute-start(bf16[1024,512]{1,0:T(8,128)(2,1)S(1)} %pad_select_fusion.3), channel_id=1, source_target_pairs={{0,4},{4,0},{8,12},{12,8},{1,5},{5,1},{9,13},{13,9},{2,6},{6,2},{1... | collective-permute-start | bytes 3145736 | tf_op jit(solution)/shard_map/ppermute | solution.py:29
  588.5 155.5 %collective-permute-start.97 = (bf16[512,1024]{1,0:T(8,128)(2,1)S(1)}, bf16[512,1024]{1,0:T(8,128)(2,1)}, u32[]{:S(2)}, u32[]{:S(2)}) collective-permute-start(bf16[512,1024]{1,0:T(8,128)(2,1)S(1)} %copy-done.17), channel_id=1, source_target_pairs={{0,16},{16,0},{1,17},{17,1},{2,18},{18,2},{3,19},{19,3},{4,20},{20... | collective-permute-start | bytes 3145736 | tf_op jit(solution)/shard_map/ppermute | solution.py:29
  588.6 32.9 %collective-permute-start.78 = (bf16[2,640,512]{2,1,0:T(8,128)(2,1)}, bf16[2,640,512]{2,1,0:T(8,128)(2,1)}, u32[]{:S(2)}, u32[]{:S(2)}) collective-permute-start(bf16[2,640,512]{2,1,0:T(8,128)(2,1)} %get-tuple-element.416), channel_id=1, source_target_pairs={{0,1},{1,0},{2,3},{3,2},{4,5},{5,4},{6,7},{7,6},{8,9},{9,8},{10,11... | collective-permute-start | bytes 3932168 | tf_op jit(solution)/shard_map/ppermute | solution.py:29
  591.4 31.2 %collective-permute-start.79 = (bf16[2,640,512]{2,1,0:T(8,128)(2,1)}, bf16[2,640,512]{2,1,0:T(8,128)(2,1)}, u32[]{:S(2)}, u32[]{:S(2)}) collective-permute-start(bf16[2,640,512]{2,1,0:T(8,128)(2,1)} %get-tuple-element.450), channel_id=1, source_target_pairs={{0,2},{1,3},{2,0},{3,1},{4,6},{5,7},{6,4},{7,5},{8,10},{9,11},{10,... | collective-permute-start | bytes 3932168 | tf_op jit(solution)/shard_map/ppermute | solution.py:29
  599.1 38.0 %collective-permute-start.77 = (bf16[768,512]{1,0:T(8,128)(2,1)S(1)}, bf16[768,512]{1,0:T(8,128)(2,1)S(1)}, u32[]{:S(2)}, u32[]{:S(2)}) collective-permute-start(bf16[768,512]{1,0:T(8,128)(2,1)S(1)} %add_convert_fusion.13), channel_id=1, source_target_pairs={{4,8},{8,4},{5,9},{9,5},{6,10},{10,6},{7,11},{11,7},{20,24},{24,20... | collective-permute-start | bytes 2359304 | tf_op jit(solution)/shard_map/ppermute | solution.py:112
  601.4 36.8 %collective-permute-start.76 = (bf16[1280,512]{1,0:T(8,128)(2,1)}, bf16[1280,512]{1,0:T(8,128)(2,1)S(1)}, u32[]{:S(2)}, u32[]{:S(2)}) collective-permute-start(bf16[1280,512]{1,0:T(8,128)(2,1)} %pad_select_fusion.1), channel_id=1, source_target_pairs={{0,4},{4,0},{8,12},{12,8},{1,5},{5,1},{9,13},{13,9},{2,6},{6,2},{1... | collective-permute-start | bytes 3932168 | tf_op jit(solution)/shard_map/ppermute | solution.py:29
  624.9 27.1 %collective-permute-start.81 = (bf16[640,512]{1,0:T(8,128)(2,1)}, bf16[640,512]{1,0:T(8,128)(2,1)}, u32[]{:S(2)}, u32[]{:S(2)}) collective-permute-start(bf16[640,512]{1,0:T(8,128)(2,1)} %fusion.17), channel_id=1, source_target_pairs={{0,1},{1,0},{2,3},{3,2},{4,5},{5,4},{6,7},{7,6},{8,9},{9,8},{10,11... | collective-permute-start | bytes 1966088 | tf_op jit(solution)/shard_map/ppermute | solution.py:29
  628.0 25.2 %collective-permute-start.80 = (bf16[640,512]{1,0:T(8,128)(2,1)}, bf16[640,512]{1,0:T(8,128)(2,1)}, u32[]{:S(2)}, u32[]{:S(2)}) collective-permute-start(bf16[640,512]{1,0:T(8,128)(2,1)} %fusion.16), channel_id=1, source_target_pairs={{0,2},{1,3},{2,0},{3,1},{4,6},{5,7},{6,4},{7,5},{8,10},{9,11},{10,... | collective-permute-start | bytes 1966088 | tf_op jit(solution)/shard_map/ppermute | solution.py:29
  638.2 26.6 %collective-permute-start.91 = (bf16[512,1024]{1,0:T(8,128)(2,1)S(1)}, bf16[512,1024]{1,0:T(8,128)(2,1)}, u32[]{:S(2)}, u32[]{:S(2)}) collective-permute-start(bf16[512,1024]{1,0:T(8,128)(2,1)S(1)} %get-tuple-element.444), channel_id=1, source_target_pairs={{4,0},{8,4},{12,8},{5,1},{9,5},{13,9},{6,2},{10,6},{14,10},{7,3},{... | collective-permute-start | bytes 3145736 | tf_op jit(solution)/shard_map/ppermute | solution.py:35
  655.8 36.0 %collective-permute-start.83 = (bf16[1024,512]{1,0:T(8,128)(2,1)S(1)}, bf16[1024,512]{1,0:T(8,128)(2,1)S(1)}, u32[]{:S(2)}, u32[]{:S(2)}) collective-permute-start(bf16[1024,512]{1,0:T(8,128)(2,1)S(1)} %add_convert_fusion.6), channel_id=1, source_target_pairs={{4,8},{8,4},{5,9},{9,5},{6,10},{10,6},{7,11},{11,7},{20,24},{24,20... | collective-permute-start | bytes 3145736 | tf_op jit(solution)/shard_map/ppermute | solution.py:112
  664.8 32.7 %collective-permute-start.82 = (bf16[1280,512]{1,0:T(8,128)(2,1)S(1)}, bf16[1280,512]{1,0:T(8,128)(2,1)S(1)}, u32[]{:S(2)}, u32[]{:S(2)}) collective-permute-start(bf16[1280,512]{1,0:T(8,128)(2,1)S(1)} %pad_select_fusion), channel_id=1, source_target_pairs={{0,4},{4,0},{8,12},{12,8},{1,5},{5,1},{9,13},{13,9},{2,6},{6,2},{1... | collective-permute-start | bytes 3932168 | tf_op jit(solution)/shard_map/ppermute | solution.py:29
  688.8 31.1 %collective-permute-start.92 = (bf16[512,1024]{1,0:T(8,128)(2,1)S(1)}, bf16[512,1024]{1,0:T(8,128)(2,1)S(1)}, u32[]{:S(2)}, u32[]{:S(2)}) collective-permute-start(bf16[512,1024]{1,0:T(8,128)(2,1)S(1)} %add_convert_fusion.4), channel_id=1, source_target_pairs={{4,0},{8,4},{12,8},{5,1},{9,5},{13,9},{6,2},{10,6},{14,10},{7,3},{... | collective-permute-start | bytes 3145736 | tf_op jit(solution)/shard_map/ppermute | solution.py:35
  690.1 33.6 %collective-permute-start.94 = (f32[2,12288]{1,0:T(2,128)S(1)}, f32[2,12288]{1,0:T(2,128)S(1)}, u32[]{:S(2)}, u32[]{:S(2)}) collective-permute-start(f32[2,12288]{1,0:T(2,128)S(1)} %fusion.41), channel_id=1, source_target_pairs={{0,1},{1,0},{2,3},{3,2},{4,5},{5,4},{6,7},{7,6},{8,9},{9,8},{10,11... | collective-permute-start | bytes 294920 | tf_op jit(solution)/shard_map/ppermute | solution.py:29
  697.9 42.1 %collective-permute-start.90 = (bf16[1280,512]{1,0:T(8,128)(2,1)S(1)}, bf16[1280,512]{1,0:T(8,128)(2,1)S(1)}, u32[]{:S(2)}, u32[]{:S(2)}) collective-permute-start(bf16[1280,512]{1,0:T(8,128)(2,1)S(1)} %add_convert_fusion.1), channel_id=1, source_target_pairs={{4,8},{8,4},{5,9},{9,5},{6,10},{10,6},{7,11},{11,7},{20,24},{24,20... | collective-permute-start | bytes 3932168 | tf_op jit(solution)/shard_map/ppermute | solution.py:112
  699.1 40.9 %collective-permute-start.89 = (bf16[1024,512]{1,0:T(8,128)(2,1)S(1)}, bf16[1024,512]{1,0:T(8,128)(2,1)S(1)}, u32[]{:S(2)}, u32[]{:S(2)}) collective-permute-start(bf16[1024,512]{1,0:T(8,128)(2,1)S(1)} %pad_select_fusion.2), channel_id=1, source_target_pairs={{0,4},{4,0},{8,12},{12,8},{1,5},{5,1},{9,13},{13,9},{2,6},{6,2},{1... | collective-permute-start | bytes 3145736 | tf_op jit(solution)/shard_map/ppermute | solution.py:29
  723.7 27.2 %collective-permute-start.98 = (f32[512,1024]{1,0:T(8,128)S(1)}, f32[512,1024]{1,0:T(8,128)S(1)}, u32[]{:S(2)}, u32[]{:S(2)}) collective-permute-start(f32[512,1024]{1,0:T(8,128)S(1)} %get-tuple-element.485), channel_id=1, source_target_pairs={{0,16},{16,0},{1,17},{17,1},{2,18},{18,2},{3,19},{19,3},{4,20},{20... | collective-permute-start | bytes 6291464 | tf_op jit(solution)/shard_map/ppermute | solution.py:29
  740.5 30.8 %collective-permute-start.95 = (bf16[1280,512]{1,0:T(8,128)(2,1)S(1)}, bf16[1280,512]{1,0:T(8,128)(2,1)S(1)}, u32[]{:S(2)}, u32[]{:S(2)}) collective-permute-start(bf16[1280,512]{1,0:T(8,128)(2,1)S(1)} %add_convert_fusion), channel_id=1, source_target_pairs={{0,4},{4,0},{8,12},{12,8},{1,5},{5,1},{9,13},{13,9},{2,6},{6,2},{1... | collective-permute-start | bytes 3932168 | tf_op jit(solution)/shard_map/ppermute | solution.py:29
  748.8 23.6 %collective-permute-start.104 = (f32[2,12288]{1,0:T(2,128)S(1)}, f32[2,12288]{1,0:T(2,128)S(1)}, u32[]{:S(2)}, u32[]{:S(2)}) collective-permute-start(f32[2,12288]{1,0:T(2,128)S(1)} %add.620), channel_id=1, source_target_pairs={{0,8},{4,12},{8,0},{12,4},{1,9},{5,13},{9,1},{13,5},{2,10},{6,14},... | collective-permute-start | bytes 294920 | tf_op jit(solution)/shard_map/ppermute | solution.py:29
  (218 other events, 2420.5 us)
where the time goes:
time: 804 us; the launch traced here: 798 us
  Pallas kernels  378 us (47%)
  waiting for transfers between devices  198 us (25%)
  starting transfers between devices  116 us (14%)
  other arithmetic  55.9 us (7%)
  local copies, waits for them, and re-layouts  46.2 us (6%)
    pallas_call x58, Pallas kernels, call(): pl.pallas_call(kernel, out_shape=out_shape, compiler_params=pltpu.Compile...  378 us
    ppermute x92, waiting for transfers between devices, flip(): return lax.ppermute(block, axis, [(i, i ^ bit) for i in range(count)])  150 us
    ppermute x92, starting transfers between devices, flip(): return lax.ppermute(block, axis, [(i, i ^ bit) for i in range(count)])  86.2 us
    ppermute x8, waiting for transfers between devices, step_along(): return lax.ppermute(block, axis, route)  47.4 us
    unnamed x337, local copies, waits for them, and re-layouts  26.9 us
    ppermute x8, starting transfers between devices, step_along(): return lax.ppermute(block, axis, route)  25.1 us
    convert_element_type x34, other arithmetic, add_bf16(): return sum((term.astype(F32) for term in terms)).astype(BF16)  17.6 us
  transfers between devices with their start and end apart: 106, of which 40 were waited for; matrix products, arithmetic and copies ran while one was open for 9% of the time, Pallas kernels for 39%

commit v1 on v0

--- a/solution.py
+++ b/solution.py
@@ -140,7 +140,7 @@
     return [pltpu.with_memory_space_constraint(array, pltpu.HBM) for array in arrays]
 
 
-def call(kernel, out_shape, *operands, limit=28, flops=0, moved=0, exps=0, name=None, **rest):
+def call(kernel, out_shape, *operands, limit=24, flops=0, moved=0, exps=0, name=None, **rest):
     return pl.pallas_call(
         kernel,
         out_shape=out_shape,

time: 804 us -> 802 us (level)
    unnamed x337 -> x327, local copies, waits for them, and re-layouts: 26.9 us -> 26.9 us
  transfers between devices with their start and end apart: 106 -> 106, of which waited for: 40 -> 39; matrix products, arithmetic and copies ran while one was open for 9% -> 8% of each run, Pallas kernels for 39% -> 39%
where the time goes in v1:
time: 802 us; the launch traced here: 796 us
  Pallas kernels  378 us (47%)
  waiting for transfers between devices  200 us (25%)
  starting transfers between devices  115 us (14%)
  other arithmetic  53.5 us (7%)
  local copies, waits for them, and re-layouts  46.3 us (6%)
    pallas_call x58, Pallas kernels, call(): pl.pallas_call(kernel, out_shape=out_shape, compiler_params=pltpu.Compile...  378 us
    ppermute x92, waiting for transfers between devices, flip(): return lax.ppermute(block, axis, [(i, i ^ bit) for i in range(count)])  152 us
    ppermute x92, starting transfers between devices, flip(): return lax.ppermute(block, axis, [(i, i ^ bit) for i in range(count)])  85.1 us
    ppermute x8, waiting for transfers between devices, step_along(): return lax.ppermute(block, axis, route)  48.1 us
    unnamed x327, local copies, waits for them, and re-layouts  26.9 us
    ppermute x8, starting transfers between devices, step_along(): return lax.ppermute(block, axis, route)  25.2 us
    convert_element_type x34, other arithmetic, add_bf16(): return sum((term.astype(F32) for term in terms)).astype(BF16)  16.2 us
  transfers between devices with their start and end apart: 106, of which 39 were waited for; matrix products, arithmetic and copies ran while one was open for 8% of the time, Pallas kernels for 39%

profile of v1, /device:TPU:0, one launch (start us, length us, event | category | flops | bytes accessed | tf_op | source)
XLA Modules:
  0.0 796.4 jit_solution(17351065112900185551)
XLA Ops:
  3.9 5.9 collective-permute-start.6
  57.3 6.2 collective-permute-done.7.own_ref
  65.7 7.5 project_qkv.2
  77.8 7.1 project_earlier.4
  84.9 7.1 project_earlier.5
  92.0 7.7 collective-permute-done.14.w1
  101.3 13.2 %attention_forward.4 = (bf16[1,512,512]{2,1,0:T(8,128)(2,1)S(1)}, bf16[1,8,512,128]{3,2,1,0:T(8,128)(2,1)}) custom-call(s32[1]{0:T(128)} %bitcast.3.me_ref.word, bf16[2,512,512]{2,1,0:T(8,128)(2,1)} %get-tuple-element.285.q_ref, bf16[2,1024,512]{2,1,0:T(8,128)(2,1)} %get-tuple-element.286.kh_ref, bf16[2,512,512]{2,1,0:T(8,128)(2,1)} %get-tuple-element.287.ko_ref, ...), custom_call_target="tpu_custom_call" | custom-call | flops 5368709120 | bytes 6291456 | tf_op jit(solution)/shard_map/attention_forward/pallas_call | solution.py:144
  123.8 13.2 %attention_forward.5 = (bf16[1,512,512]{2,1,0:T(8,128)(2,1)S(1)}, bf16[1,8,512,128]{3,2,1,0:T(8,128)(2,1)}) custom-call(s32[1]{0:T(128)} %bitcast.3.me_ref.word, bf16[2,512,512]{2,1,0:T(8,128)(2,1)} %get-tuple-element.285.q_ref, bf16[2,1024,512]{2,1,0:T(8,128)(2,1)} %get-tuple-element.286.kh_ref, bf16[2,512,512]{2,1,0:T(8,128)(2,1)} %get-tuple-element.287.ko_ref, ...), custom_call_target="tpu_custom_call" | custom-call | flops 5368709120 | bytes 6291456 | tf_op jit(solution)/shard_map/attention_forward/pallas_call | solution.py:144
  143.6 6.6 up.6
  150.3 6.3 up.7
  172.0 14.4 %collective-permute-done.26.w1.refs_4_.refs_5_ = bf16[1024,512]{1,0:T(8,128)(2,1)S(1)} collective-permute-done((bf16[1024,512]{1,0:T(8,128)(2,1)S(1)}, bf16[1024,512]{1,0:T(8,128)(2,1)S(1)}, u32[]{:S(2)}, u32[]{:S(2)}) %collective-permute-start.26) | collective-permute-done | bytes 1048608 | tf_op jit(solution)/shard_map/ppermute | solution.py:29
  205.8 7.7 project_qkv.3
  213.6 6.5 collective-permute-done.31.own_ref
  224.2 7.0 project_earlier.6
  231.2 7.0 project_earlier.7
  238.2 7.8 collective-permute-done.34.w1
  247.0 13.2 %attention_forward.6 = (bf16[1,512,512]{2,1,0:T(8,128)(2,1)S(1)}, bf16[1,8,512,128]{3,2,1,0:T(8,128)(2,1)}) custom-call(s32[1]{0:T(128)} %bitcast.3.me_ref.word, bf16[2,512,512]{2,1,0:T(8,128)(2,1)} %get-tuple-element.317.q_ref, bf16[2,1024,512]{2,1,0:T(8,128)(2,1)} %get-tuple-element.318.kh_ref, bf16[2,512,512]{2,1,0:T(8,128)(2,1)} %get-tuple-element.319.ko_ref, ...), custom_call_target="tpu_custom_call" | custom-call | flops 5368709120 | bytes 6291456 | tf_op jit(solution)/shard_map/attention_forward/pallas_call | solution.py:144
  269.5 12.8 %attention_forward.7 = (bf16[1,512,512]{2,1,0:T(8,128)(2,1)S(1)}, bf16[1,8,512,128]{3,2,1,0:T(8,128)(2,1)}) custom-call(s32[1]{0:T(128)} %bitcast.3.me_ref.word, bf16[2,512,512]{2,1,0:T(8,128)(2,1)} %get-tuple-element.317.q_ref, bf16[2,1024,512]{2,1,0:T(8,128)(2,1)} %get-tuple-element.318.kh_ref, bf16[2,512,512]{2,1,0:T(8,128)(2,1)} %get-tuple-element.319.ko_ref, ...), custom_call_target="tpu_custom_call" | custom-call | flops 5368709120 | bytes 6291456 | tf_op jit(solution)/shard_map/attention_forward/pallas_call | solution.py:144
  289.3 6.7 up.8
  296.0 6.3 up.9
  313.7 7.8 act_back.2
  329.6 9.3 %down_grad.2 = (bf16[2,512,512]{2,1,0:T(8,128)(2,1)}, bf16[2,512,512]{2,1,0:T(8,128)(2,1)}, bf16[2,512,512]{2,1,0:T(8,128)(2,1)}, bf16[2,512,512]{2,1,0:T(8,128)(2,1)}) custom-call(s32[4]{0:T(128)S(1)} %pad_add_fusion.order, bf16[512,2048]{1,0:T(8,128)(2,1)} %copy-done.48, bf16[512,2048]{1,0:T(8,128)(2,1)} %copy-done.107, bf16[512,1024]{1,0:T(8,128)(2,1)S(1)} %copy-done.26, ...), custom_call_target="tpu_custom_call" | custom-call | flops 4294967296 | bytes 10485760 | tf_op jit(solution)/shard_map/down_grad/pallas_call | solution.py:144
  339.1 6.0 middle_back.2
  351.1 9.8 %up_grad.2 = (bf16[2,640,512]{2,1,0:T(8,128)(2,1)}, bf16[2,640,512]{2,1,0:T(8,128)(2,1)}, bf16[2,640,512]{2,1,0:T(8,128)(2,1)}, bf16[2,640,512]{2,1,0:T(8,128)(2,1)}) custom-call(s32[4]{0:T(128)S(1)} %pad_add_fusion.order, bf16[512,1024]{1,0:T(8,128)(2,1)S(1)} %copy-done.101, bf16[512,1024]{1,0:T(8,128)(2,1)S(1)} %copy-done.103, ...), custom_call_target="tpu_custom_call" | custom-call | flops 5368709120 | bytes 14680064 | tf_op jit(solution)/shard_map/up_grad/pallas_call | solution.py:144
  360.9 12.4 %attention_backward.8 = (f32[1,512,512]{2,1,0:T(8,128)S(1)}, bf16[1,1024,512]{2,1,0:T(8,128)(2,1)S(1)}, bf16[1,1024,512]{2,1,0:T(8,128)(2,1)S(1)}) custom-call(s32[1]{0:T(128)} %bitcast.3.me_ref.word, bf16[2,512,512]{2,1,0:T(8,128)(2,1)} %get-tuple-element.317.q_ref, bf16[2,1024,512]{2,1,0:T(8,128)(2,1)} %get-tuple-element.318.kh_ref, ...), custom_call_target="tpu_custom_call" | custom-call | flops 8053062656 | bytes 8388608 | tf_op jit(solution)/shard_map/attention_backward/pallas_call | solution.py:144
  383.2 12.3 %attention_backward.9 = (f32[1,512,512]{2,1,0:T(8,128)S(1)}, bf16[1,1024,512]{2,1,0:T(8,128)(2,1)S(1)}, bf16[1,1024,512]{2,1,0:T(8,128)(2,1)S(1)}) custom-call(s32[1]{0:T(128)} %bitcast.3.me_ref.word, bf16[2,512,512]{2,1,0:T(8,128)(2,1)} %get-tuple-element.317.q_ref, bf16[2,1024,512]{2,1,0:T(8,128)(2,1)} %get-tuple-element.318.kh_ref, ...), custom_call_target="tpu_custom_call" | custom-call | flops 8053062656 | bytes 8388608 | tf_op jit(solution)/shard_map/attention_backward/pallas_call | solution.py:144
  403.2 7.8 attention_backward.10
  414.4 7.2 collective-permute-done.52
  424.4 7.8 attention_backward.11
  434.0 12.5 %qkv_grad.2 = (bf16[2,384,512]{2,1,0:T(8,128)(2,1)}, bf16[2,384,512]{2,1,0:T(8,128)(2,1)}, bf16[2,384,512]{2,1,0:T(8,128)(2,1)}, bf16[2,384,512]{2,1,0:T(8,128)(2,1)}, f32[8,512]{1,0:T(8,128)S(1)}) custom-call(s32[4]{0:T(128)S(1)} %pad_add_fusion.order, bf16[2,512,1024]{2,1,0:T(8,128)(2,1)S(1)} %copy-done.15, bf16[2,1024,1024]{2,1,0:T(8,128)(2,1)S(1)} %copy-done.9, ...), custom_call_target="tpu_custom_call" | custom-call | flops 7516192768 | bytes 16777216 | tf_op jit(solution)/shard_map/qkv_grad/pallas_call | solution.py:144
  450.6 10.3 %collective-permute-done.57.got = bf16[512,1024]{1,0:T(8,128)(2,1)S(1)} collective-permute-done((bf16[512,1024]{1,0:T(8,128)(2,1)S(1)}, bf16[512,1024]{1,0:T(8,128)(2,1)S(1)}, u32[]{:S(2)}, u32[]{:S(2)}) %collective-permute-start.57) | collective-permute-done | bytes 1048608 | tf_op jit(solution)/shard_map/ppermute | solution.py:35
  483.8 8.2 %act_back.3 = (bf16[512,2048]{1,0:T(8,128)(2,1)S(1)}, bf16[512,2048]{1,0:T(8,128)(2,1)S(1)}, f32[8,2048]{1,0:T(8,128)S(1)}) custom-call(s32[1]{0:T(128)} %bitcast.3.me_ref.word, bf16[512,1024]{1,0:T(8,128)(2,1)S(1)} %copy-done.29, bf16[512,1024]{1,0:T(8,128)(2,1)} %collective-permute-done.62.other, bf16[512,2048]{1,0:T(8,128)(2,1)} %get-tuple-element.404.slope_own, ...), custom_call_target="tpu_custom_call" | custom-call | flops 4294967296 | bytes 16777216 | tf_op jit(solution)/shard_map/act_back/pallas_call | solution.py:144
  502.3 9.8 %down_grad.3 = (bf16[2,512,512]{2,1,0:T(8,128)(2,1)}, bf16[2,512,512]{2,1,0:T(8,128)(2,1)}, bf16[2,512,512]{2,1,0:T(8,128)(2,1)}, bf16[2,512,512]{2,1,0:T(8,128)(2,1)}) custom-call(s32[4]{0:T(128)S(1)} %copy-done.95, bf16[512,2048]{1,0:T(8,128)(2,1)} %copy-done.45, bf16[512,2048]{1,0:T(8,128)(2,1)} %copy-done.104, bf16[512,1024]{1,0:T(8,128)(2,1)S(1)} %copy-done.30, ...), custom_call_target="tpu_custom_call" | custom-call | flops 4294967296 | bytes 10485760 | tf_op jit(solution)/shard_map/down_grad/pallas_call | solution.py:144
  522.3 9.8 %up_grad.3 = (bf16[2,640,512]{2,1,0:T(8,128)(2,1)}, bf16[2,640,512]{2,1,0:T(8,128)(2,1)}, bf16[2,640,512]{2,1,0:T(8,128)(2,1)}, bf16[2,640,512]{2,1,0:T(8,128)(2,1)}) custom-call(s32[4]{0:T(128)S(1)} %copy-done.95, bf16[512,1024]{1,0:T(8,128)(2,1)S(1)} %copy-done.97, bf16[512,1024]{1,0:T(8,128)(2,1)S(1)} %copy-done.99, ...), custom_call_target="tpu_custom_call" | custom-call | flops 5368709120 | bytes 14680064 | tf_op jit(solution)/shard_map/up_grad/pallas_call | solution.py:144
  533.3 12.4 %attention_backward.12 = (f32[1,512,512]{2,1,0:T(8,128)S(1)}, bf16[1,1024,512]{2,1,0:T(8,128)(2,1)S(1)}, bf16[1,1024,512]{2,1,0:T(8,128)(2,1)S(1)}) custom-call(s32[1]{0:T(128)} %bitcast.3.me_ref.word, bf16[2,512,512]{2,1,0:T(8,128)(2,1)} %get-tuple-element.285.q_ref, bf16[2,1024,512]{2,1,0:T(8,128)(2,1)} %get-tuple-element.286.kh_ref, ...), custom_call_target="tpu_custom_call" | custom-call | flops 8053062656 | bytes 8388608 | tf_op jit(solution)/shard_map/attention_backward/pallas_call | solution.py:144
  547.1 15.8 %collective-permute-done.65 = bf16[1280,512]{1,0:T(8,128)(2,1)S(1)} collective-permute-done((bf16[1280,512]{1,0:T(8,128)(2,1)S(1)}, bf16[1280,512]{1,0:T(8,128)(2,1)S(1)}, u32[]{:S(2)}, u32[]{:S(2)}) %collective-permute-start.65) | collective-permute-done | bytes 1310752 | tf_op jit(solution)/shard_map/ppermute | solution.py:29
  576.3 12.5 %attention_backward.13 = (f32[1,512,512]{2,1,0:T(8,128)S(1)}, bf16[1,1024,512]{2,1,0:T(8,128)(2,1)S(1)}, bf16[1,1024,512]{2,1,0:T(8,128)(2,1)S(1)}) custom-call(s32[1]{0:T(128)} %bitcast.3.me_ref.word, bf16[2,512,512]{2,1,0:T(8,128)(2,1)} %get-tuple-element.285.q_ref, bf16[2,1024,512]{2,1,0:T(8,128)(2,1)} %get-tuple-element.286.kh_ref, ...), custom_call_target="tpu_custom_call" | custom-call | flops 8053062656 | bytes 8388608 | tf_op jit(solution)/shard_map/attention_backward/pallas_call | solution.py:144
  600.8 8.8 %collective-permute-start.76 = (bf16[1280,512]{1,0:T(8,128)(2,1)S(1)}, bf16[1280,512]{1,0:T(8,128)(2,1)S(1)}, u32[]{:S(2)}, u32[]{:S(2)}) collective-permute-start(bf16[1280,512]{1,0:T(8,128)(2,1)S(1)} %pad_select_fusion.1), channel_id=1, source_target_pairs={{0,4},{4,0},{8,12},{12,8},{1,5},{5,1},{9,13},{13,9},{2,6},{6,2},{1... | collective-permute-start | bytes 3932168 | tf_op jit(solution)/shard_map/ppermute | solution.py:29
  609.6 7.8 attention_backward.14
  628.3 7.8 attention_backward.15
  638.7 12.5 %qkv_grad.3 = (bf16[2,384,512]{2,1,0:T(8,128)(2,1)}, bf16[2,384,512]{2,1,0:T(8,128)(2,1)}, bf16[2,384,512]{2,1,0:T(8,128)(2,1)}, bf16[2,384,512]{2,1,0:T(8,128)(2,1)}, f32[8,512]{1,0:T(8,128)S(1)}) custom-call(s32[4]{0:T(128)S(1)} %copy-done.95, bf16[2,512,1024]{2,1,0:T(8,128)(2,1)S(1)} %copy-done.14, bf16[2,1024,1024]{2,1,0:T(8,128)(2,1)S(1)} %copy-done.8, ...), custom_call_target="tpu_custom_call" | custom-call | flops 7516192768 | bytes 16777216 | tf_op jit(solution)/shard_map/qkv_grad/pallas_call | solution.py:144
  670.2 7.9 collective-permute-done.85
  680.4 7.0 collective-permute-done.88
  690.3 6.5 collective-permute-done.82
  700.6 18.7 %collective-permute-done.92.got = bf16[512,1024]{1,0:T(8,128)(2,1)S(1)} collective-permute-done((bf16[512,1024]{1,0:T(8,128)(2,1)S(1)}, bf16[512,1024]{1,0:T(8,128)(2,1)S(1)}, u32[]{:S(2)}, u32[]{:S(2)}) %collective-permute-start.92) | collective-permute-done | bytes 1048608 | tf_op jit(solution)/shard_map/ppermute | solution.py:35
  728.6 10.3 %collective-permute-done.89 = bf16[1024,512]{1,0:T(8,128)(2,1)S(1)} collective-permute-done((bf16[1024,512]{1,0:T(8,128)(2,1)S(1)}, bf16[1024,512]{1,0:T(8,128)(2,1)S(1)}, u32[]{:S(2)}, u32[]{:S(2)}) %collective-permute-start.89) | collective-permute-done | bytes 1048608 | tf_op jit(solution)/shard_map/ppermute | solution.py:29
  753.3 16.9 %collective-permute-done.95 = bf16[1280,512]{1,0:T(8,128)(2,1)S(1)} collective-permute-done((bf16[1280,512]{1,0:T(8,128)(2,1)S(1)}, bf16[1280,512]{1,0:T(8,128)(2,1)S(1)}, u32[]{:S(2)}, u32[]{:S(2)}) %collective-permute-start.95) | collective-permute-done | bytes 1310752 | tf_op jit(solution)/shard_map/ppermute | solution.py:29
  777.8 13.8 %collective-permute-done.101 = bf16[768,512]{1,0:T(8,128)(2,1)S(1)} collective-permute-done((bf16[768,512]{1,0:T(8,128)(2,1)S(1)}, bf16[768,512]{1,0:T(8,128)(2,1)S(1)}, u32[]{:S(2)}, u32[]{:S(2)}) %collective-permute-start.101) | collective-permute-done | bytes 786464 | tf_op jit(solution)/shard_map/ppermute | solution.py:29
  (680 shorter events, 332.5 us)
Async XLA Ops:
  3.9 34.5 %collective-permute-start.6 = (bf16[512,1024]{1,0:T(8,128)(2,1)}, bf16[512,1024]{1,0:T(8,128)(2,1)}, u32[]{:S(2)}, u32[]{:S(2)}) collective-permute-start(bf16[512,1024]{1,0:T(8,128)(2,1)} %get-tuple-element.564.own_ref.x_ref), channel_id=1, source_target_pairs={{0,4},{4,8},{8,12},{1,5},{5,9},{9,13},{2,6},{6,10},{10,14},{3,7},{... | collective-permute-start | bytes 3145736 | tf_op jit(solution)/shard_map/ppermute | solution.py:35
  19.6 28.7 %collective-permute-start.8 = (bf16[1024,512]{1,0:T(8,128)(2,1)S(1)}, bf16[1024,512]{1,0:T(8,128)(2,1)S(1)}, u32[]{:S(2)}, u32[]{:S(2)}) collective-permute-start(bf16[1024,512]{1,0:T(8,128)(2,1)S(1)} %get-tuple-element.562.w0.refs_3_.refs_4_), channel_id=1, source_target_pairs={{0,1},{1,0},{2,3},{3,2},{4,5},{5,4},{6,7},{7,6},{8,9},{9,8},{10,11... | collective-permute-start | bytes 3145736 | tf_op jit(solution)/shard_map/ppermute | solution.py:29
  21.2 28.5 %collective-permute-start.9 = (bf16[1024,512]{1,0:T(8,128)(2,1)S(1)}, bf16[1024,512]{1,0:T(8,128)(2,1)}, u32[]{:S(2)}, u32[]{:S(2)}) collective-permute-start(bf16[1024,512]{1,0:T(8,128)(2,1)S(1)} %get-tuple-element.562.w0.refs_3_.refs_4_), channel_id=1, source_target_pairs={{0,2},{1,3},{2,0},{3,1},{4,6},{5,7},{6,4},{7,5},{8,10},{9,11},{10,... | collective-permute-start | bytes 3145736 | tf_op jit(solution)/shard_map/ppermute | solution.py:29
  38.3 25.2 %collective-permute-start.7 = (bf16[512,1024]{1,0:T(8,128)(2,1)}, bf16[512,1024]{1,0:T(8,128)(2,1)}, u32[]{:S(2)}, u32[]{:S(2)}) collective-permute-start(bf16[512,1024]{1,0:T(8,128)(2,1)} %collective-permute-done.6.own_ref), channel_id=1, source_target_pairs={{0,4},{4,8},{8,12},{1,5},{5,9},{9,13},{2,6},{6,10},{10,14},{3,7},{... | collective-permute-start | bytes 3145736 | tf_op jit(solution)/shard_map/ppermute | solution.py:35
  73.7 26.0 %collective-permute-start.14 = (bf16[1024,512]{1,0:T(8,128)(2,1)S(1)}, bf16[1024,512]{1,0:T(8,128)(2,1)S(1)}, u32[]{:S(2)}, u32[]{:S(2)}) collective-permute-start(bf16[1024,512]{1,0:T(8,128)(2,1)S(1)} %copy-done.18), channel_id=1, source_target_pairs={{0,1},{1,0},{2,3},{3,2},{4,5},{5,4},{6,7},{7,6},{8,9},{9,8},{10,11... | collective-permute-start | bytes 3145736 | tf_op jit(solution)/shard_map/ppermute | solution.py:29
  75.2 26.1 %collective-permute-start.15 = (bf16[1024,512]{1,0:T(8,128)(2,1)S(1)}, bf16[1024,512]{1,0:T(8,128)(2,1)S(1)}, u32[]{:S(2)}, u32[]{:S(2)}) collective-permute-start(bf16[1024,512]{1,0:T(8,128)(2,1)S(1)} %copy-done.18), channel_id=1, source_target_pairs={{0,2},{1,3},{2,0},{3,1},{4,6},{5,7},{6,4},{7,5},{8,10},{9,11},{10,... | collective-permute-start | bytes 3145736 | tf_op jit(solution)/shard_map/ppermute | solution.py:29
  76.8 44.7 %collective-permute-start.16 = (bf16[1024,512]{1,0:T(8,128)(2,1)S(1)}, bf16[1024,512]{1,0:T(8,128)(2,1)S(1)}, u32[]{:S(2)}, u32[]{:S(2)}) collective-permute-start(bf16[1024,512]{1,0:T(8,128)(2,1)S(1)} %copy-done.20), channel_id=1, source_target_pairs={{0,1},{1,0},{2,3},{3,2},{4,5},{5,4},{6,7},{7,6},{8,9},{9,8},{10,11... | collective-permute-start | bytes 3145736 | tf_op jit(solution)/shard_map/ppermute | solution.py:29
  77.3 46.5 %collective-permute-start.17 = (bf16[1024,512]{1,0:T(8,128)(2,1)S(1)}, bf16[1024,512]{1,0:T(8,128)(2,1)S(1)}, u32[]{:S(2)}, u32[]{:S(2)}) collective-permute-start(bf16[1024,512]{1,0:T(8,128)(2,1)S(1)} %copy-done.20), channel_id=1, source_target_pairs={{0,2},{1,3},{2,0},{3,1},{4,6},{5,7},{6,4},{7,5},{8,10},{9,11},{10,... | collective-permute-start | bytes 3145736 | tf_op jit(solution)/shard_map/ppermute | solution.py:29
  160.9 25.5 %collective-permute-start.26 = (bf16[1024,512]{1,0:T(8,128)(2,1)S(1)}, bf16[1024,512]{1,0:T(8,128)(2,1)S(1)}, u32[]{:S(2)}, u32[]{:S(2)}) collective-permute-start(bf16[1024,512]{1,0:T(8,128)(2,1)S(1)} %get-tuple-element.305.w0.refs_3_.refs_4_), channel_id=1, source_target_pairs={{0,1},{1,0},{2,3},{3,2},{4,5},{5,4},{6,7},{7,6},{8,9},{9,8},{10,11... | collective-permute-start | bytes 3145736 | tf_op jit(solution)/shard_map/ppermute | solution.py:29
  161.9 25.9 %collective-permute-start.27 = (bf16[1024,512]{1,0:T(8,128)(2,1)S(1)}, bf16[1024,512]{1,0:T(8,128)(2,1)S(1)}, u32[]{:S(2)}, u32[]{:S(2)}) collective-permute-start(bf16[1024,512]{1,0:T(8,128)(2,1)S(1)} %get-tuple-element.305.w0.refs_3_.refs_4_), channel_id=1, source_target_pairs={{0,2},{1,3},{2,0},{3,1},{4,6},{5,7},{6,4},{7,5},{8,10},{9,11},{10,... | collective-permute-start | bytes 3145736 | tf_op jit(solution)/shard_map/ppermute | solution.py:29
  167.1 26.7 %collective-permute-start.30 = (bf16[512,1024]{1,0:T(8,128)(2,1)}, bf16[512,1024]{1,0:T(8,128)(2,1)}, u32[]{:S(2)}, u32[]{:S(2)}) collective-permute-start(bf16[512,1024]{1,0:T(8,128)(2,1)} %down_own.2.own_ref.x_ref), channel_id=1, source_target_pairs={{0,4},{4,8},{8,12},{1,5},{5,9},{9,13},{2,6},{6,10},{10,14},{3,7},{... | collective-permute-start | bytes 3145736 | tf_op jit(solution)/shard_map/ppermute | solution.py:35
  172.0 30.6 %collective-permute-start.25 = (bf16[512,1024]{1,0:T(8,128)(2,1)}, bf16[512,1024]{1,0:T(8,128)(2,1)}, u32[]{:S(2)}, u32[]{:S(2)}) collective-permute-start(bf16[512,1024]{1,0:T(8,128)(2,1)} %down_own.2.own_ref.x_ref), channel_id=1, source_target_pairs={{0,16},{16,0},{1,17},{17,1},{2,18},{18,2},{3,19},{19,3},{4,20},{20... | collective-permute-start | bytes 3145736 | tf_op jit(solution)/shard_map/ppermute | solution.py:29
  193.8 26.3 %collective-permute-start.31 = (bf16[512,1024]{1,0:T(8,128)(2,1)}, bf16[512,1024]{1,0:T(8,128)(2,1)}, u32[]{:S(2)}, u32[]{:S(2)}) collective-permute-start(bf16[512,1024]{1,0:T(8,128)(2,1)} %collective-permute-done.30.own_ref), channel_id=1, source_target_pairs={{0,4},{4,8},{8,12},{1,5},{5,9},{9,13},{2,6},{6,10},{10,14},{3,7},{... | collective-permute-start | bytes 3145736 | tf_op jit(solution)/shard_map/ppermute | solution.py:35
  220.1 26.0 %collective-permute-start.34 = (bf16[1024,512]{1,0:T(8,128)(2,1)S(1)}, bf16[1024,512]{1,0:T(8,128)(2,1)S(1)}, u32[]{:S(2)}, u32[]{:S(2)}) collective-permute-start(bf16[1024,512]{1,0:T(8,128)(2,1)S(1)} %copy-done.22), channel_id=1, source_target_pairs={{0,1},{1,0},{2,3},{3,2},{4,5},{5,4},{6,7},{7,6},{8,9},{9,8},{10,11... | collective-permute-start | bytes 3145736 | tf_op jit(solution)/shard_map/ppermute | solution.py:29
  221.0 26.0 %collective-permute-start.35 = (bf16[1024,512]{1,0:T(8,128)(2,1)S(1)}, bf16[1024,512]{1,0:T(8,128)(2,1)S(1)}, u32[]{:S(2)}, u32[]{:S(2)}) collective-permute-start(bf16[1024,512]{1,0:T(8,128)(2,1)S(1)} %copy-done.22), channel_id=1, source_target_pairs={{0,2},{1,3},{2,0},{3,1},{4,6},{5,7},{6,4},{7,5},{8,10},{9,11},{10,... | collective-permute-start | bytes 3145736 | tf_op jit(solution)/shard_map/ppermute | solution.py:29
  222.5 46.0 %collective-permute-start.36 = (bf16[1024,512]{1,0:T(8,128)(2,1)S(1)}, bf16[1024,512]{1,0:T(8,128)(2,1)S(1)}, u32[]{:S(2)}, u32[]{:S(2)}) collective-permute-start(bf16[1024,512]{1,0:T(8,128)(2,1)S(1)} %copy-done.24), channel_id=1, source_target_pairs={{0,1},{1,0},{2,3},{3,2},{4,5},{5,4},{6,7},{7,6},{8,9},{9,8},{10,11... | collective-permute-start | bytes 3145736 | tf_op jit(solution)/shard_map/ppermute | solution.py:29
  223.5 46.0 %collective-permute-start.37 = (bf16[1024,512]{1,0:T(8,128)(2,1)S(1)}, bf16[1024,512]{1,0:T(8,128)(2,1)S(1)}, u32[]{:S(2)}, u32[]{:S(2)}) collective-permute-start(bf16[1024,512]{1,0:T(8,128)(2,1)S(1)} %copy-done.24), channel_id=1, source_target_pairs={{0,2},{1,3},{2,0},{3,1},{4,6},{5,7},{6,4},{7,5},{8,10},{9,11},{10,... | collective-permute-start | bytes 3145736 | tf_op jit(solution)/shard_map/ppermute | solution.py:29
  345.6 27.7 %collective-permute-start.45 = (bf16[2,512,512]{2,1,0:T(8,128)(2,1)S(1)}, bf16[2,512,512]{2,1,0:T(8,128)(2,1)S(1)}, u32[]{:S(2)}, u32[]{:S(2)}) collective-permute-start(bf16[2,512,512]{2,1,0:T(8,128)(2,1)S(1)} %copy-done.153), channel_id=1, source_target_pairs={{0,1},{1,0},{2,3},{3,2},{4,5},{5,4},{6,7},{7,6},{8,9},{9,8},{10,11... | collective-permute-start | bytes 3145736 | tf_op jit(solution)/shard_map/ppermute | solution.py:29
  346.7 26.7 %collective-permute-start.46 = (bf16[2,512,512]{2,1,0:T(8,128)(2,1)S(1)}, bf16[2,512,512]{2,1,0:T(8,128)(2,1)S(1)}, u32[]{:S(2)}, u32[]{:S(2)}) collective-permute-start(bf16[2,512,512]{2,1,0:T(8,128)(2,1)S(1)} %copy-done.152), channel_id=1, source_target_pairs={{0,2},{1,3},{2,0},{3,1},{4,6},{5,7},{6,4},{7,5},{8,10},{9,11},{10,... | collective-permute-start | bytes 3145736 | tf_op jit(solution)/shard_map/ppermute | solution.py:29
  381.1 40.4 %collective-permute-start.52 = (bf16[2,640,512]{2,1,0:T(8,128)(2,1)S(1)}, bf16[2,640,512]{2,1,0:T(8,128)(2,1)S(1)}, u32[]{:S(2)}, u32[]{:S(2)}) collective-permute-start(bf16[2,640,512]{2,1,0:T(8,128)(2,1)S(1)} %copy-done.149), channel_id=1, source_target_pairs={{0,1},{1,0},{2,3},{3,2},{4,5},{5,4},{6,7},{7,6},{8,9},{9,8},{10,11... | collective-permute-start | bytes 3932168 | tf_op jit(solution)/shard_map/ppermute | solution.py:29
  382.2 40.1 %collective-permute-start.53 = (bf16[2,640,512]{2,1,0:T(8,128)(2,1)S(1)}, bf16[2,640,512]{2,1,0:T(8,128)(2,1)S(1)}, u32[]{:S(2)}, u32[]{:S(2)}) collective-permute-start(bf16[2,640,512]{2,1,0:T(8,128)(2,1)S(1)} %copy-done.148), channel_id=1, source_target_pairs={{0,2},{1,3},{2,0},{3,1},{4,6},{5,7},{6,4},{7,5},{8,10},{9,11},{10,... | collective-permute-start | bytes 3932168 | tf_op jit(solution)/shard_map/ppermute | solution.py:29
  401.8 30.4 %collective-permute-start.54 = (bf16[512,1024]{1,0:T(8,128)(2,1)S(1)}, bf16[512,1024]{1,0:T(8,128)(2,1)S(1)}, u32[]{:S(2)}, u32[]{:S(2)}) collective-permute-start(bf16[512,1024]{1,0:T(8,128)(2,1)S(1)} %get-tuple-element.371), channel_id=1, source_target_pairs={{4,0},{8,4},{12,8},{5,1},{9,5},{13,9},{6,2},{10,6},{14,10},{7,3},{... | collective-permute-start | bytes 3145736 | tf_op jit(solution)/shard_map/ppermute | solution.py:35
  422.5 24.9 %collective-permute-start.56 = (bf16[640,512]{1,0:T(8,128)(2,1)S(1)}, bf16[640,512]{1,0:T(8,128)(2,1)S(1)}, u32[]{:S(2)}, u32[]{:S(2)}) collective-permute-start(bf16[640,512]{1,0:T(8,128)(2,1)S(1)} %fusion.15), channel_id=1, source_target_pairs={{0,1},{1,0},{2,3},{3,2},{4,5},{5,4},{6,7},{7,6},{8,9},{9,8},{10,11... | collective-permute-start | bytes 1966088 | tf_op jit(solution)/shard_map/ppermute | solution.py:29
  424.4 36.5 %collective-permute-start.58 = (bf16[512,1024]{1,0:T(8,128)(2,1)S(1)}, bf16[512,1024]{1,0:T(8,128)(2,1)S(1)}, u32[]{:S(2)}, u32[]{:S(2)}) collective-permute-start(bf16[512,1024]{1,0:T(8,128)(2,1)S(1)} %get-tuple-element.377), channel_id=1, source_target_pairs={{0,16},{16,0},{1,17},{17,1},{2,18},{18,2},{3,19},{19,3},{4,20},{20... | collective-permute-start | bytes 3145736 | tf_op jit(solution)/shard_map/ppermute | solution.py:29
  432.6 28.2 %collective-permute-start.57 = (bf16[512,1024]{1,0:T(8,128)(2,1)S(1)}, bf16[512,1024]{1,0:T(8,128)(2,1)S(1)}, u32[]{:S(2)}, u32[]{:S(2)}) collective-permute-start(bf16[512,1024]{1,0:T(8,128)(2,1)S(1)} %add_convert_fusion.9), channel_id=1, source_target_pairs={{4,0},{8,4},{12,8},{5,1},{9,5},{13,9},{6,2},{10,6},{14,10},{7,3},{... | collective-permute-start | bytes 3145736 | tf_op jit(solution)/shard_map/ppermute | solution.py:35
  495.7 36.5 %collective-permute-start.61 = (bf16[1024,512]{1,0:T(8,128)(2,1)S(1)}, bf16[1024,512]{1,0:T(8,128)(2,1)S(1)}, u32[]{:S(2)}, u32[]{:S(2)}) collective-permute-start(bf16[1024,512]{1,0:T(8,128)(2,1)S(1)} %copy-done.109), channel_id=1, source_target_pairs={{0,4},{4,0},{8,12},{12,8},{1,5},{5,1},{9,13},{13,9},{2,6},{6,2},{1... | collective-permute-start | bytes 3145736 | tf_op jit(solution)/shard_map/ppermute | solution.py:29
  516.9 28.8 %collective-permute-start.71 = (bf16[2,512,512]{2,1,0:T(8,128)(2,1)S(1)}, bf16[2,512,512]{2,1,0:T(8,128)(2,1)S(1)}, u32[]{:S(2)}, u32[]{:S(2)}) collective-permute-start(bf16[2,512,512]{2,1,0:T(8,128)(2,1)S(1)} %copy-done.151), channel_id=1, source_target_pairs={{0,1},{1,0},{2,3},{3,2},{4,5},{5,4},{6,7},{7,6},{8,9},{9,8},{10,11... | collective-permute-start | bytes 3145736 | tf_op jit(solution)/shard_map/ppermute | solution.py:29
  518.1 27.6 %collective-permute-start.72 = (bf16[2,512,512]{2,1,0:T(8,128)(2,1)S(1)}, bf16[2,512,512]{2,1,0:T(8,128)(2,1)S(1)}, u32[]{:S(2)}, u32[]{:S(2)}) collective-permute-start(bf16[2,512,512]{2,1,0:T(8,128)(2,1)S(1)} %copy-done.150), channel_id=1, source_target_pairs={{0,2},{1,3},{2,0},{3,1},{4,6},{5,7},{6,4},{7,5},{8,10},{9,11},{10,... | collective-permute-start | bytes 3145736 | tf_op jit(solution)/shard_map/ppermute | solution.py:29
  532.1 30.8 %collective-permute-start.65 = (bf16[1280,512]{1,0:T(8,128)(2,1)S(1)}, bf16[1280,512]{1,0:T(8,128)(2,1)S(1)}, u32[]{:S(2)}, u32[]{:S(2)}) collective-permute-start(bf16[1280,512]{1,0:T(8,128)(2,1)S(1)} %copy-done.108), channel_id=1, source_target_pairs={{0,4},{4,0},{8,12},{12,8},{1,5},{5,1},{9,13},{13,9},{2,6},{6,2},{1... | collective-permute-start | bytes 3932168 | tf_op jit(solution)/shard_map/ppermute | solution.py:29
  570.9 28.3 %collective-permute-start.70 = (bf16[1280,512]{1,0:T(8,128)(2,1)S(1)}, bf16[1280,512]{1,0:T(8,128)(2,1)S(1)}, u32[]{:S(2)}, u32[]{:S(2)}) collective-permute-start(bf16[1280,512]{1,0:T(8,128)(2,1)S(1)} %add_convert_fusion.3), channel_id=1, source_target_pairs={{4,8},{8,4},{5,9},{9,5},{6,10},{10,6},{7,11},{11,7},{20,24},{24,20... | collective-permute-start | bytes 3932168 | tf_op jit(solution)/shard_map/ppermute | solution.py:112
  571.7 27.6 %collective-permute-start.69 = (bf16[1024,512]{1,0:T(8,128)(2,1)S(1)}, bf16[1024,512]{1,0:T(8,128)(2,1)S(1)}, u32[]{:S(2)}, u32[]{:S(2)}) collective-permute-start(bf16[1024,512]{1,0:T(8,128)(2,1)S(1)} %pad_select_fusion.3), channel_id=1, source_target_pairs={{0,4},{4,0},{8,12},{12,8},{1,5},{5,1},{9,13},{13,9},{2,6},{6,2},{1... | collective-permute-start | bytes 3145736 | tf_op jit(solution)/shard_map/ppermute | solution.py:29
  588.8 153.6 %collective-permute-start.97 = (bf16[512,1024]{1,0:T(8,128)(2,1)S(1)}, bf16[512,1024]{1,0:T(8,128)(2,1)}, u32[]{:S(2)}, u32[]{:S(2)}) collective-permute-start(bf16[512,1024]{1,0:T(8,128)(2,1)S(1)} %copy-done.17), channel_id=1, source_target_pairs={{0,16},{16,0},{1,17},{17,1},{2,18},{18,2},{3,19},{19,3},{4,20},{20... | collective-permute-start | bytes 3145736 | tf_op jit(solution)/shard_map/ppermute | solution.py:29
  588.9 32.0 %collective-permute-start.78 = (bf16[2,640,512]{2,1,0:T(8,128)(2,1)}, bf16[2,640,512]{2,1,0:T(8,128)(2,1)}, u32[]{:S(2)}, u32[]{:S(2)}) collective-permute-start(bf16[2,640,512]{2,1,0:T(8,128)(2,1)} %get-tuple-element.416), channel_id=1, source_target_pairs={{0,1},{1,0},{2,3},{3,2},{4,5},{5,4},{6,7},{7,6},{8,9},{9,8},{10,11... | collective-permute-start | bytes 3932168 | tf_op jit(solution)/shard_map/ppermute | solution.py:29
  590.6 31.2 %collective-permute-start.79 = (bf16[2,640,512]{2,1,0:T(8,128)(2,1)}, bf16[2,640,512]{2,1,0:T(8,128)(2,1)}, u32[]{:S(2)}, u32[]{:S(2)}) collective-permute-start(bf16[2,640,512]{2,1,0:T(8,128)(2,1)} %get-tuple-element.450), channel_id=1, source_target_pairs={{0,2},{1,3},{2,0},{3,1},{4,6},{5,7},{6,4},{7,5},{8,10},{9,11},{10,... | collective-permute-start | bytes 3932168 | tf_op jit(solution)/shard_map/ppermute | solution.py:29
  599.5 36.7 %collective-permute-start.77 = (bf16[768,512]{1,0:T(8,128)(2,1)S(1)}, bf16[768,512]{1,0:T(8,128)(2,1)S(1)}, u32[]{:S(2)}, u32[]{:S(2)}) collective-permute-start(bf16[768,512]{1,0:T(8,128)(2,1)S(1)} %add_convert_fusion.13), channel_id=1, source_target_pairs={{4,8},{8,4},{5,9},{9,5},{6,10},{10,6},{7,11},{11,7},{20,24},{24,20... | collective-permute-start | bytes 2359304 | tf_op jit(solution)/shard_map/ppermute | solution.py:112
  600.8 36.6 %collective-permute-start.76 = (bf16[1280,512]{1,0:T(8,128)(2,1)S(1)}, bf16[1280,512]{1,0:T(8,128)(2,1)S(1)}, u32[]{:S(2)}, u32[]{:S(2)}) collective-permute-start(bf16[1280,512]{1,0:T(8,128)(2,1)S(1)} %pad_select_fusion.1), channel_id=1, source_target_pairs={{0,4},{4,0},{8,12},{12,8},{1,5},{5,1},{9,13},{13,9},{2,6},{6,2},{1... | collective-permute-start | bytes 3932168 | tf_op jit(solution)/shard_map/ppermute | solution.py:29
  623.9 27.3 %collective-permute-start.81 = (bf16[640,512]{1,0:T(8,128)(2,1)}, bf16[640,512]{1,0:T(8,128)(2,1)S(1)}, u32[]{:S(2)}, u32[]{:S(2)}) collective-permute-start(bf16[640,512]{1,0:T(8,128)(2,1)} %fusion.17), channel_id=1, source_target_pairs={{0,1},{1,0},{2,3},{3,2},{4,5},{5,4},{6,7},{7,6},{8,9},{9,8},{10,11... | collective-permute-start | bytes 1966088 | tf_op jit(solution)/shard_map/ppermute | solution.py:29
  627.0 25.2 %collective-permute-start.80 = (bf16[640,512]{1,0:T(8,128)(2,1)}, bf16[640,512]{1,0:T(8,128)(2,1)}, u32[]{:S(2)}, u32[]{:S(2)}) collective-permute-start(bf16[640,512]{1,0:T(8,128)(2,1)} %fusion.16), channel_id=1, source_target_pairs={{0,2},{1,3},{2,0},{3,1},{4,6},{5,7},{6,4},{7,5},{8,10},{9,11},{10,... | collective-permute-start | bytes 1966088 | tf_op jit(solution)/shard_map/ppermute | solution.py:29
  637.4 26.4 %collective-permute-start.91 = (bf16[512,1024]{1,0:T(8,128)(2,1)S(1)}, bf16[512,1024]{1,0:T(8,128)(2,1)}, u32[]{:S(2)}, u32[]{:S(2)}) collective-permute-start(bf16[512,1024]{1,0:T(8,128)(2,1)S(1)} %get-tuple-element.444), channel_id=1, source_target_pairs={{4,0},{8,4},{12,8},{5,1},{9,5},{13,9},{6,2},{10,6},{14,10},{7,3},{... | collective-permute-start | bytes 3145736 | tf_op jit(solution)/shard_map/ppermute | solution.py:35
  654.7 35.6 %collective-permute-start.83 = (bf16[1024,512]{1,0:T(8,128)(2,1)S(1)}, bf16[1024,512]{1,0:T(8,128)(2,1)S(1)}, u32[]{:S(2)}, u32[]{:S(2)}) collective-permute-start(bf16[1024,512]{1,0:T(8,128)(2,1)S(1)} %add_convert_fusion.6), channel_id=1, source_target_pairs={{4,8},{8,4},{5,9},{9,5},{6,10},{10,6},{7,11},{11,7},{20,24},{24,20... | collective-permute-start | bytes 3145736 | tf_op jit(solution)/shard_map/ppermute | solution.py:112
  663.8 33.0 %collective-permute-start.82 = (bf16[1280,512]{1,0:T(8,128)(2,1)S(1)}, bf16[1280,512]{1,0:T(8,128)(2,1)S(1)}, u32[]{:S(2)}, u32[]{:S(2)}) collective-permute-start(bf16[1280,512]{1,0:T(8,128)(2,1)S(1)} %pad_select_fusion), channel_id=1, source_target_pairs={{0,4},{4,0},{8,12},{12,8},{1,5},{5,1},{9,13},{13,9},{2,6},{6,2},{1... | collective-permute-start | bytes 3932168 | tf_op jit(solution)/shard_map/ppermute | solution.py:29
  687.3 32.0 %collective-permute-start.92 = (bf16[512,1024]{1,0:T(8,128)(2,1)S(1)}, bf16[512,1024]{1,0:T(8,128)(2,1)S(1)}, u32[]{:S(2)}, u32[]{:S(2)}) collective-permute-start(bf16[512,1024]{1,0:T(8,128)(2,1)S(1)} %add_convert_fusion.4), channel_id=1, source_target_pairs={{4,0},{8,4},{12,8},{5,1},{9,5},{13,9},{6,2},{10,6},{14,10},{7,3},{... | collective-permute-start | bytes 3145736 | tf_op jit(solution)/shard_map/ppermute | solution.py:35
  688.6 34.4 %collective-permute-start.94 = (f32[2,12288]{1,0:T(2,128)S(1)}, f32[2,12288]{1,0:T(2,128)S(1)}, u32[]{:S(2)}, u32[]{:S(2)}) collective-permute-start(f32[2,12288]{1,0:T(2,128)S(1)} %fusion.41), channel_id=1, source_target_pairs={{0,1},{1,0},{2,3},{3,2},{4,5},{5,4},{6,7},{7,6},{8,9},{9,8},{10,11... | collective-permute-start | bytes 294920 | tf_op jit(solution)/shard_map/ppermute | solution.py:29
  697.2 41.7 %collective-permute-start.90 = (bf16[1280,512]{1,0:T(8,128)(2,1)S(1)}, bf16[1280,512]{1,0:T(8,128)(2,1)S(1)}, u32[]{:S(2)}, u32[]{:S(2)}) collective-permute-start(bf16[1280,512]{1,0:T(8,128)(2,1)S(1)} %add_convert_fusion.1), channel_id=1, source_target_pairs={{4,8},{8,4},{5,9},{9,5},{6,10},{10,6},{7,11},{11,7},{20,24},{24,20... | collective-permute-start | bytes 3932168 | tf_op jit(solution)/shard_map/ppermute | solution.py:112
  698.4 40.5 %collective-permute-start.89 = (bf16[1024,512]{1,0:T(8,128)(2,1)S(1)}, bf16[1024,512]{1,0:T(8,128)(2,1)S(1)}, u32[]{:S(2)}, u32[]{:S(2)}) collective-permute-start(bf16[1024,512]{1,0:T(8,128)(2,1)S(1)} %pad_select_fusion.2), channel_id=1, source_target_pairs={{0,4},{4,0},{8,12},{12,8},{1,5},{5,1},{9,13},{13,9},{2,6},{6,2},{1... | collective-permute-start | bytes 3145736 | tf_op jit(solution)/shard_map/ppermute | solution.py:29
  723.1 26.2 %collective-permute-start.98 = (f32[512,1024]{1,0:T(8,128)S(1)}, f32[512,1024]{1,0:T(8,128)S(1)}, u32[]{:S(2)}, u32[]{:S(2)}) collective-permute-start(f32[512,1024]{1,0:T(8,128)S(1)} %get-tuple-element.485), channel_id=1, source_target_pairs={{0,16},{16,0},{1,17},{17,1},{2,18},{18,2},{3,19},{19,3},{4,20},{20... | collective-permute-start | bytes 6291464 | tf_op jit(solution)/shard_map/ppermute | solution.py:29
  739.3 30.8 %collective-permute-start.95 = (bf16[1280,512]{1,0:T(8,128)(2,1)S(1)}, bf16[1280,512]{1,0:T(8,128)(2,1)S(1)}, u32[]{:S(2)}, u32[]{:S(2)}) collective-permute-start(bf16[1280,512]{1,0:T(8,128)(2,1)S(1)} %add_convert_fusion), channel_id=1, source_target_pairs={{0,4},{4,0},{8,12},{12,8},{1,5},{5,1},{9,13},{13,9},{2,6},{6,2},{1... | collective-permute-start | bytes 3932168 | tf_op jit(solution)/shard_map/ppermute | solution.py:29
  747.1 24.1 %collective-permute-start.104 = (f32[2,12288]{1,0:T(2,128)S(1)}, f32[2,12288]{1,0:T(2,128)S(1)}, u32[]{:S(2)}, u32[]{:S(2)}) collective-permute-start(f32[2,12288]{1,0:T(2,128)S(1)} %add.620), channel_id=1, source_target_pairs={{0,8},{4,12},{8,0},{12,4},{1,9},{5,13},{9,1},{13,5},{2,10},{6,14},... | collective-permute-start | bytes 294920 | tf_op jit(solution)/shard_map/ppermute | solution.py:29
  (213 other events, 2376.8 us)
